TPU v7x, 128 devices: a whole 4x4x4 slice. The times are simulated.
128 devices in a mesh: section: 2 (over core), fsdp: 16 (over x, z), rep: 4 (over y).
Axes of the slice: x: 4, y: 4, z: 4, core: 2. Of those that a mesh axis runs over, the one named last changes fastest.
Arguments:
- layer_in: bfloat16 [2, 64, 64, 768], P(None, ('fsdp', 'rep')), may hold values from -6 to 6
- cotangent: bfloat16 [2, 64, 64, 768], P(None, ('fsdp', 'rep')), may hold values from -6 to 6
- encoder: bfloat16 [2, 64, 256, 768], P(None, ('fsdp', 'rep')), may hold values from -6 to 6
- dec_segments: int32 [2, 64, 64], P(None, ('fsdp', 'rep')), may hold values from 0 to 3, as said below
- enc_segments: int32 [2, 64, 256], P(None, ('fsdp', 'rep')), may hold values from 0 to 3, as said below
- norm_gains: bfloat16 [2, 3, 768], P('section', None, 'fsdp'), may hold values from 0.5 to 1.5
- self_query: bfloat16 [2, 768, 768], P('section', 'fsdp'), may hold values from -0.02734375 to 0.02734375
- self_kv: bfloat16 [2, 768, 2, 768], P('section', 'fsdp'), may hold values from -0.21875 to 0.21875
- self_out: bfloat16 [2, 768, 768], P('section', 'fsdp'), may hold values from -0.875 to 0.875
- rel_bias: bfloat16 [2, 32, 12], P('section', 'fsdp'), may hold values from -6 to 6
- cross_query: bfloat16 [2, 768, 768], P('section', 'fsdp'), may hold values from -0.02734375 to 0.02734375
- cross_kv: bfloat16 [2, 768, 2, 768], P('section', 'fsdp'), may hold values from -0.21875 to 0.21875
- cross_out: bfloat16 [2, 768, 768], P('section', 'fsdp'), may hold values from -1.25 to 1.25
- ffn_in: bfloat16 [2, 768, 2, 2048], P('section', 'fsdp'), may hold values from -0.21875 to 0.21875
- ffn_out: bfloat16 [2, 2048, 768], P('section', 'fsdp'), may hold values from -0.25 to 0.25
Outputs:
- layer_out: bfloat16 [2, 2, 64, 64, 768], P('section', None, ('fsdp', 'rep'))
- layer_grad: bfloat16 [2, 2, 64, 64, 768], P('section', None, ('fsdp', 'rep'))
- encoder_grad: float32 [2, 64, 256, 768], P(None, ('fsdp', 'rep'))
- grad_norm_gains: float32 [2, 3, 768], P('section', None, 'fsdp')
- grad_self_query: float32 [2, 768, 768], P('section', 'fsdp')
- grad_self_kv: float32 [2, 768, 2, 768], P('section', 'fsdp')
- grad_self_out: float32 [2, 768, 768], P('section', 'fsdp')
- grad_rel_bias: float32 [2, 32, 12], P('section', 'fsdp')
- grad_cross_query: float32 [2, 768, 768], P('section', 'fsdp')
- grad_cross_kv: float32 [2, 768, 2, 768], P('section', 'fsdp')
- grad_cross_out: float32 [2, 768, 768], P('section', 'fsdp')
- grad_ffn_in: float32 [2, 768, 2, 2048], P('section', 'fsdp')
- grad_ffn_out: float32 [2, 2048, 768], P('section', 'fsdp')
Inputs may be any that keep to these rules, and one draw needn't show every extreme that they name: `dec_segments`: within each packed row the ids start at 0 and rise by one at each of 3 places, so every id of 0 to 3 is present. `enc_segments`: within each row of encoder states the ids start at 0 and rise by one at each of 3 places, so every id of 0 to 3 is present.
All inputs are finite; a program needn't handle non-finite values.
Results may differ from a plain program's by a relative error of at most 0.035.
Values may be sent and summed in bfloat16 or wider, within the bound.
No kernel may reach another device: no remote copies, remote signals or barrier semaphores. Data moves between devices by JAX's collectives and lax.ppermute only.
A program may use at most 128 MiB of HBM per device.

v0:
```python
import jax
import jax.numpy as jnp
import numpy as np
from jax import lax
from jax.experimental import pallas as pl
from jax.experimental.pallas import tpu as pltpu
from jax.sharding import PartitionSpec as P

HEADS = 12
HEAD = 64
BUCKETS = 32
MAX_DIST = 128
PARTS = 16
GELU_SCALE = float(np.sqrt(2.0 / np.pi))


epsilon = 1e-06
highest = lax.Precision.HIGHEST


def bucket_row(length):
    distance = np.arange(length)
    half_count = BUCKETS // 2
    scaled = (
        np.log(np.maximum(distance, half_count) / half_count)
        / np.log(MAX_DIST / half_count)
        * (BUCKETS - half_count)
    )
    far_bucket = np.minimum(half_count + np.floor(scaled).astype(np.int32), BUCKETS - 1)
    return np.where(distance < half_count, distance, far_bucket).astype(np.int32)


def bucket_onehot(length):
    return (bucket_row(length)[None, :] == np.arange(BUCKETS)[:, None]).astype(np.float32)


def spread_distance(by_distance):
    head_count, length = by_distance.shape
    padded_row = jnp.concatenate(
        [jnp.zeros((head_count, length - 1), jnp.float32), by_distance], axis=1
    )
    tiled = jnp.tile(padded_row, (1, length))
    tiled = jnp.concatenate([tiled, jnp.zeros((head_count, length), jnp.float32)], axis=1)
    return tiled.reshape(head_count, length, 2 * length)[:, :, :length][:, :, ::-1]


def gather_distance(grid):
    head_count, length, _ = grid.shape
    flipped = jnp.concatenate(
        [grid[:, :, ::-1], jnp.zeros((head_count, length, length), jnp.float32)], axis=2
    )
    flat = flipped.reshape(head_count, 2 * length * length)[:, : length * (2 * length - 1)]
    return jnp.sum(flat.reshape(head_count, length, 2 * length - 1), axis=1)[:, length - 1 :]


ROWS_OWN = 48
TOKENS = 64
WIDE = 768
FF = 2048
GROUP = 256
GROUPS = 3
BATCHES = 2
STATES = 256
CHUNK = 512
CHUNKS = FF // CHUNK
ATT = 6144
ALL_TOKENS = (BATCHES * TOKENS, WIDE)
ALL_STATES = (BATCHES * STATES, WIDE)
HIDDEN = (BATCHES * TOKENS, FF)
VMEM_BYTES = 60 * 1024 * 1024
FULL = (PARTS, ROWS_OWN, WIDE)
GATED = (PARTS, ROWS_OWN, FF)
DOWN = (PARTS, FF // PARTS, WIDE)
RING = 4
LATE_HIDDEN = [name + str(index) for index in range(1, CHUNKS) for name in ("gate", "up")]
DOWN_PIECES = [(piece, block) for piece in range(GROUPS) for block in range(8)]


def product(left, right, along_left=1, along_right=0):
    return lax.dot_general(
        left,
        right,
        (((along_left,), (along_right,)), ((), ())),
        preferred_element_type=jnp.float32,
    )


def low(value):
    return value.astype(jnp.bfloat16)


def same_head():
    row = lax.broadcasted_iota(jnp.int32, (GROUP, GROUP), 0) // HEAD
    lane = lax.broadcasted_iota(jnp.int32, (GROUP, GROUP), 1) // HEAD
    return jnp.where(row == lane, 1.0, 0.0)


def spread_heads(block, own_low):
    return jnp.concatenate([block] * 4, axis=0) * own_low


def fold_heads(block, own):
    kept = block * own
    return kept[:64] + kept[64:128] + kept[128:192] + kept[192:]


def scale_of(value):
    return lax.rsqrt(jnp.mean(value * value, axis=-1, keepdims=True) + epsilon)


def norm_back(grad, value, gain):
    scale = scale_of(value)
    carried = grad * gain
    mean = jnp.mean(value * carried, axis=-1, keepdims=True)
    grad_value = carried * scale - value * (scale * scale * scale) * mean
    grad_gain = jnp.sum(grad * value * scale, axis=0, keepdims=True)
    return grad_value, grad_gain


def square(ref):
    return ref[...].reshape(WIDE, WIDE)


def down_at(ref, piece, block):
    return ref.at[:, 1, pl.ds(16 * piece, 16), pl.ds(2 * FF + GROUP * block, GROUP)]


def rows_at(ref, piece, block):
    return ref.at[:, pl.ds(16 * block, 16), pl.ds(GROUP * piece, GROUP)]


def softmax_rows(scores):
    raised = jnp.exp(scores - jnp.max(scores, axis=-1, keepdims=True))
    return raised / jnp.sum(raised, axis=-1, keepdims=True)


def gelu_parts(gate):
    cube = gate * gate * gate
    bent = jnp.tanh(GELU_SCALE * (gate + 0.044715 * cube))
    half = 0.5 * (1.0 + bent)
    slope = half + 0.5 * gate * (1.0 - bent * bent) * GELU_SCALE * (
        1.0 + 3.0 * 0.044715 * gate * gate
    )
    return gate * half, slope


def weight_copies(weight, slots, sems):
    copies = {}
    for place, (name, column) in enumerate(
        (("q", 0), ("k", 1), ("v", 2), ("o", 3), ("cq", 4), ("ck", 5), ("cv", 6), ("co", 7))
    ):
        if name in slots:
            source = weight.at[:, 0, :, pl.ds(WIDE * column, WIDE)]
            copies[name] = [pltpu.make_async_copy(source, slots[name], sems.at[place])]
    for place, (name, column) in enumerate((("gate", 0), ("up", FF))):
        if name in slots:
            for index in range(CHUNKS):
                start = CHUNK * index
                source = weight.at[:, 1, :, pl.ds(column + start, CHUNK)]
                target = slots[name].at[:, :, pl.ds(start, CHUNK)]
                sem = sems.at[8 + CHUNKS * place + index]
                copies[name + str(index)] = [pltpu.make_async_copy(source, target, sem)]
    if "down" in slots:
        copies["down"] = [
            pltpu.make_async_copy(
                down_at(weight, piece, block),
                rows_at(slots["down"], piece, block),
                sems.at[8 + 2 * CHUNKS + place],
            )
            for place, (piece, block) in enumerate(DOWN_PIECES)
        ]
    return copies


def begin(copies, names):
    for name in names:
        for copy in copies[name]:
            copy.start()


def finish(copies, name):
    for copy in copies[name]:
        copy.wait()


def forward_body(
    keys_given,
    x_ref,
    enc_ref,
    self_add_ref,
    cross_add_ref,
    gains_ref,
    weight,
    out_ref,
    n1_ref,
    q_ref,
    k_ref,
    v_ref,
    p_ref,
    o_ref,
    a2_ref,
    n2_ref,
    cq_ref,
    ck_ref,
    cv_ref,
    cp_ref,
    co_ref,
    a3_ref,
    n3_ref,
    gate_ref,
    up_ref,
    hid_ref,
    wq,
    wk,
    wv,
    wo,
    wcq,
    wck,
    wcv,
    wco,
    wg,
    wu,
    wd,
    sems,
):
    slots = dict(q=wq, k=wk, v=wv, o=wo, cq=wcq, co=wco, gate=wg, up=wu, down=wd)
    if not keys_given:
        slots.update(ck=wck, cv=wcv)
    copies = weight_copies(weight, slots, sems)
    if not keys_given:
        begin(copies, ("ck", "cv"))
    begin(copies, ("q", "k", "v", "o", "cq", "co", "gate0", "up0", "down", *LATE_HIDDEN))
    own = same_head()
    own_low = low(own)
    stream = x_ref[...].astype(jnp.float32)
    normed = low(stream * scale_of(stream) * gains_ref[0:1])
    n1_ref[...] = normed
    if not keys_given:
        for name, held_weight, target in (("ck", wck, ck_ref), ("cv", wcv, cv_ref)):
            finish(copies, name)
            for row in range(BATCHES):
                part = pl.ds(STATES * row, STATES)
                target[part] = low(product(enc_ref[part], square(held_weight)))
    finish(copies, "q")
    q_ref[...] = low(product(normed, square(wq)))
    finish(copies, "k")
    k_ref[...] = low(product(normed, square(wk)))
    finish(copies, "v")
    v_ref[...] = low(product(normed, square(wv)))
    for row in range(BATCHES):
        part = pl.ds(TOKENS * row, TOKENS)
        for group in range(GROUPS):
            lanes = pl.ds(GROUP * group, GROUP)
            spread = spread_heads(q_ref[part, lanes], own_low)
            scores = product(spread, k_ref[part, lanes], 1, 1) + self_add_ref[row, lanes]
            chance = softmax_rows(scores)
            p_ref[row, lanes] = chance
            mixed = product(low(chance), v_ref[part, lanes])
            o_ref[part, lanes] = low(fold_heads(mixed, own))
    finish(copies, "o")
    stream = stream + product(o_ref[...], square(wo))
    a2_ref[...] = stream
    normed = low(stream * scale_of(stream) * gains_ref[1:2])
    n2_ref[...] = normed
    finish(copies, "cq")
    cq_ref[...] = low(product(normed, square(wcq)))
    for row in range(BATCHES):
        part = pl.ds(TOKENS * row, TOKENS)
        keys = pl.ds(STATES * row, STATES)
        add = jnp.concatenate([cross_add_ref[row]] * 4, axis=0)
        for group in range(GROUPS):
            lanes = pl.ds(GROUP * group, GROUP)
            spread = spread_heads(cq_ref[part, lanes], own_low)
            scores = product(spread, ck_ref[keys, lanes], 1, 1) + add
            chance = softmax_rows(scores)
            cp_ref[row, lanes] = chance
            mixed = product(low(chance), cv_ref[keys, lanes])
            co_ref[part, lanes] = low(fold_heads(mixed, own))
    finish(copies, "co")
    stream = a2_ref[...] + product(co_ref[...], square(wco))
    a3_ref[...] = stream
    n3_ref[...] = low(stream * scale_of(stream) * gains_ref[2:3])
    total = a3_ref[...]
    for index in range(CHUNKS):
        lanes = pl.ds(index * CHUNK, CHUNK)
        rows = n3_ref[...]
        finish(copies, "gate" + str(index))
        gate = product(rows, wg[:, :, lanes].reshape(WIDE, CHUNK))
        finish(copies, "up" + str(index))
        up = product(rows, wu[:, :, lanes].reshape(WIDE, CHUNK))
        gate_ref[:, lanes] = gate
        up_ref[:, lanes] = up
        bent = 0.5 * (1.0 + jnp.tanh(GELU_SCALE * (gate + 0.044715 * (gate * gate * gate))))
        hidden = low(gate * bent * up)
        hid_ref[:, lanes] = hidden
        if index == 0:
            finish(copies, "down")
        total = total + product(hidden, wd[pl.ds(4 * index, 4)].reshape(CHUNK, WIDE))
    out_ref[...] = low(total)


def first_kernel(
    x_ref, enc_ref, self_add_ref, cross_add_ref, gains_ref, weight, out_ref, ck_ref, cv_ref, *rest
):
    (n1, q, k, v, p, o, a2, n2, cq, cp, co, a3, n3, gate, up, hid, *scratch) = rest
    forward_body(
        False,
        x_ref, enc_ref, self_add_ref, cross_add_ref, gains_ref, weight, out_ref,
        n1, q, k, v, p, o, a2, n2, cq, ck_ref, cv_ref, cp, co, a3, n3, gate, up, hid, *scratch,
    )


def turn_kernel(
    x_ref, ck_ref, cv_ref, self_add_ref, cross_add_ref, gains_ref, c_ref, weight,
    out_ref, da_ref, *rest,
):
    saved_out, saved, rest = rest[:16], rest[16:32], rest[32:]
    dc_ref, dcq_ref, dck_ref, dcv_ref, dself_ref, dq_ref, dk_ref, dv_ref, *rest = rest
    wq, wk, wv, wo, wcq, wco, wg, wu, wd, sems, out_sems = rest
    n1, q, k, v, p, o, a2, n2, cq, cp, co, a3, n3, gate, up, hid = saved
    forward_body(
        True,
        x_ref, None, self_add_ref, cross_add_ref, gains_ref, weight, out_ref,
        n1, q, k, v, p, o, a2, n2, cq, ck_ref, cv_ref, cp, co, a3, n3, gate, up, hid,
        wq, wk, wv, wo, wcq, None, None, wco, wg, wu, wd, sems,
    )
    sent = [
        pltpu.make_async_copy(source, target, out_sems.at[place])
        for place, (source, target) in enumerate(zip(saved, saved_out))
    ]
    for copy in sent:
        copy.start()

    def finish_weight(name):
        return None

    def emit(index, lanes, dgate, dup):
        return None

    stream, _ = hidden_back(finish_weight, emit, c_ref, a3, gains_ref, gate, up, wg, wu, wd)
    stream, _ = cross_back(
        stream, finish_weight, gains_ref, a2, cq, ck_ref, cv_ref, cp, wcq, wco,
        dc_ref, dcq_ref, dck_ref, dcv_ref,
    )
    stream, _ = self_back(
        stream, finish_weight, gains_ref, x_ref, q, k, v, p, wq, wk, wv, wo,
        dself_ref, dq_ref, dk_ref, dv_ref, None,
    )
    da_ref[...] = low(stream)
    for copy in sent:
        copy.wait()


def core_is(part):
    return lax.axis_index("section") == part


def push(source, keep, send, part, window, sem):
    @pl.when(core_is(part))
    def _():
        pltpu.make_async_copy(source, keep.at[window], sem).start()

    @pl.when(jnp.logical_not(core_is(part)))
    def _():
        pltpu.make_async_copy(source, send.at[window], sem).start()

    return pltpu.make_async_copy(source, keep.at[window], sem)


def columns(start, width):
    return (slice(None), slice(None), slice(None), pl.ds(start, width))


def put_square(slot, part, lanes, value):
    value = value.reshape(RING, RING, ROWS_OWN, value.shape[-1])
    if part == 1:
        slot[:, :, :, lanes] = value
    else:
        for place in range(RING):
            slot[:, place, :, lanes] = value[place]


def hidden_back(finish_weight, emit, c_ref, a3_ref, gains_ref, gate_ref, up_ref, wg, wu, wd):
    total = jnp.zeros(ALL_TOKENS, jnp.float32)
    finish_weight("down")
    for index in range(CHUNKS):
        lanes = pl.ds(index * CHUNK, CHUNK)
        grad = product(c_ref[...], wd[pl.ds(4 * index, 4)].reshape(CHUNK, WIDE), 1, 1)
        bent, slope = gelu_parts(gate_ref[:, lanes])
        dgate = low(grad * up_ref[:, lanes] * slope)
        dup = low(grad * bent)
        finish_weight("gate" + str(index))
        total = total + product(dgate, wg[:, :, lanes].reshape(WIDE, CHUNK), 1, 1)
        finish_weight("up" + str(index))
        total = total + product(dup, wu[:, :, lanes].reshape(WIDE, CHUNK), 1, 1)
        emit(index, lanes, dgate, dup)
    back, dgain = norm_back(total, a3_ref[...], gains_ref[2:3])
    return c_ref[...].astype(jnp.float32) + back, dgain


def cross_back(
    stream, finish_weight, gains_ref, a2_ref, cq_ref, ck_ref, cv_ref, cp_ref, wcq, wco,
    dc_ref, dcq_ref, dck_ref, dcv_ref,
):
    own = same_head()
    own_low = low(own)
    dc_ref[...] = low(stream)
    finish_weight("co")
    datt = low(product(dc_ref[...], square(wco), 1, 1))
    for row in range(BATCHES):
        part = pl.ds(TOKENS * row, TOKENS)
        keys = pl.ds(STATES * row, STATES)
        for group in range(GROUPS):
            lanes = pl.ds(GROUP * group, GROUP)
            left = GROUP * group
            dout = spread_heads(
                datt[TOKENS * row : TOKENS * (row + 1), left : left + GROUP], own_low
            )
            spread = spread_heads(cq_ref[part, lanes], own_low)
            chance = cp_ref[row, lanes]
            dchance = product(dout, cv_ref[keys, lanes], 1, 1)
            dcv_ref[keys, lanes] = low(product(low(chance), dout, 0, 0))
            inner = jnp.sum(chance * dchance, axis=-1, keepdims=True)
            dscore = low(chance * (dchance - inner))
            dcq_ref[part, lanes] = low(fold_heads(product(dscore, ck_ref[keys, lanes]), own))
            dck_ref[keys, lanes] = low(product(dscore, spread, 0, 0))
    finish_weight("cq")
    grad = product(dcq_ref[...], square(wcq), 1, 1)
    back, dgain = norm_back(grad, a2_ref[...], gains_ref[1:2])
    return stream + back, dgain


def self_back(
    stream, finish_weight, gains_ref, x_ref, q_ref, k_ref, v_ref, p_ref, wq, wk, wv, wo,
    dself_ref, dq_ref, dk_ref, dv_ref, dscore_ref,
):
    own = same_head()
    own_low = low(own)
    dself_ref[...] = low(stream)
    finish_weight("o")
    datt = low(product(dself_ref[...], square(wo), 1, 1))
    for row in range(BATCHES):
        part = pl.ds(TOKENS * row, TOKENS)
        for group in range(GROUPS):
            lanes = pl.ds(GROUP * group, GROUP)
            left = GROUP * group
            dout = spread_heads(
                datt[TOKENS * row : TOKENS * (row + 1), left : left + GROUP], own_low
            )
            spread = spread_heads(q_ref[part, lanes], own_low)
            chance = p_ref[row, lanes]
            dchance = product(dout, v_ref[part, lanes], 1, 1)
            dv_ref[part, lanes] = low(product(low(chance), dout, 0, 0))
            inner = jnp.sum(chance * dchance, axis=-1, keepdims=True)
            dscore = low(chance * (dchance - inner))
            if dscore_ref is not None:
                if row == 0:
                    dscore_ref[lanes] = dscore.astype(jnp.float32)
                else:
                    dscore_ref[lanes] += dscore.astype(jnp.float32)
            dq_ref[part, lanes] = low(fold_heads(product(dscore, k_ref[part, lanes]), own))
            dk_ref[part, lanes] = low(product(dscore, spread, 0, 0))
    finish_weight("q")
    grad = product(dq_ref[...], square(wq), 1, 1)
    finish_weight("k")
    grad = grad + product(dk_ref[...], square(wk), 1, 1)
    finish_weight("v")
    grad = grad + product(dv_ref[...], square(wv), 1, 1)
    back, dgain = norm_back(grad, x_ref[...].astype(jnp.float32), gains_ref[0:1])
    return stream + back, dgain


def hidden_kernel(
    c_ref, a3_ref, gains_ref, gate_ref, up_ref, n3_ref, hid_ref, weight,
    stream_ref, dgain_ref, keep, send,
    wg, wu, wd, gg, gu, gd0, gd1, sems, out_sems,
):
    copies = weight_copies(weight, dict(gate=wg, up=wu, down=wd), sems)
    begin(copies, ("down", "gate0", "up0", *LATE_HIDDEN))
    sent = []

    def finish_weight(name):
        finish(copies, name)

    for index in range(RING):
        lanes = pl.ds(index * CHUNK, CHUNK)
        grad = low(product(hid_ref[:, lanes], c_ref[...], 0, 0))
        grad = grad.reshape(RING, FF // PARTS, WIDE)
        gd0[:, index] = grad[:, : FF // PARTS // 2]
        gd1[index] = grad[:, FF // PARTS // 2 :]
    for part, tall in enumerate((gd0, gd1)):
        for piece in range(GROUPS):
            for block in range(4):
                source = tall.at[:, :, pl.ds(16 * block, 16), pl.ds(GROUP * piece, GROUP)]
                window = (
                    slice(None),
                    slice(None),
                    pl.ds(16 * piece, 16),
                    pl.ds(FF + GROUP * block, GROUP),
                )
                sent.append(push(source, keep, send, part, window, out_sems.at[len(sent)]))

    def emit(index, lanes, dgate, dup):
        for part, slot, grad in ((0, gg, dgate), (1, gu, dup)):
            put_square(slot, part, lanes, low(product(n3_ref[...], grad, 0, 0)))
            window = columns(index * CHUNK, CHUNK)
            sent.append(
                push(slot.at[window], keep, send, part, window, out_sems.at[len(sent)])
            )

    stream, dgain = hidden_back(
        finish_weight, emit, c_ref, a3_ref, gains_ref, gate_ref, up_ref, wg, wu, wd
    )
    stream_ref[...] = stream
    dgain_ref[...] = dgain
    for copy in sent:
        copy.wait()


def cross_kernel(
    stream_ref, gains_ref, a2_ref, cq_ref, ck_ref, cv_ref, cp_ref, weight,
    next_ref, dgain_ref, dc_ref, dcq_ref, dck_ref, dcv_ref,
    wcq, wco, sems,
):
    copies = weight_copies(weight, dict(cq=wcq, co=wco), sems)
    begin(copies, ("co", "cq"))

    def finish_weight(name):
        finish(copies, name)

    stream, dgain = cross_back(
        stream_ref[...], finish_weight, gains_ref, a2_ref, cq_ref, ck_ref, cv_ref, cp_ref,
        wcq, wco, dc_ref, dcq_ref, dck_ref, dcv_ref,
    )
    next_ref[...] = stream
    dgain_ref[...] = dgain


def self_kernel(
    stream_ref, x_ref, gains_ref, q_ref, k_ref, v_ref, p_ref,
    enc_ref, n1_ref, o_ref, n2_ref, co_ref, dc_ref, dcq_ref, dck_ref, dcv_ref, weight,
    da_ref, dgain_ref, dscore_ref, denc_ref, keep, send,
    dself_ref, dq_ref, dk_ref, dv_ref,
    wq, wk, wv, wo, wck, wcv, g0, g1, g2, g3, g4, g5, g6, g7, sems, out_sems,
):
    slots = dict(q=wq, k=wk, v=wv, o=wo, ck=wck, cv=wcv)
    copies = weight_copies(weight, slots, sems)
    begin(copies, ("o", "q", "k", "v", "ck", "cv"))

    def finish_weight(name):
        finish(copies, name)

    sent = []

    def emit(slot, part, column, left, right):
        put_square(slot, part, slice(None), low(product(left[...], right[...], 0, 0)))
        window = columns(WIDE * column, WIDE)
        sent.append(push(slot, keep, send, part, window, out_sems.at[len(sent)]))

    emit(g0, 0, 0, co_ref, dc_ref)
    emit(g1, 0, 1, n2_ref, dcq_ref)
    emit(g2, 1, 0, enc_ref, dck_ref)
    emit(g3, 1, 1, enc_ref, dcv_ref)
    stream, dgain = self_back(
        stream_ref[...], finish_weight, gains_ref, x_ref, q_ref, k_ref, v_ref, p_ref,
        wq, wk, wv, wo, dself_ref, dq_ref, dk_ref, dv_ref, dscore_ref,
    )
    da_ref[...] = low(stream)
    dgain_ref[...] = dgain
    emit(g4, 0, 2, o_ref, dself_ref)
    emit(g5, 0, 3, n1_ref, dq_ref)
    emit(g6, 1, 2, n1_ref, dk_ref)
    emit(g7, 1, 3, n1_ref, dv_ref)
    finish(copies, "ck")
    finish(copies, "cv")
    for row in range(BATCHES):
        keys = pl.ds(STATES * row, STATES)
        denc_ref[keys] = low(
            product(dck_ref[keys], square(wck), 1, 1) + product(dcv_ref[keys], square(wcv), 1, 1)
        )
    for copy in sent:
        copy.wait()


def in_vmem(count):
    return [pl.BlockSpec(memory_space=pltpu.VMEM)] * count


def held(*shapes):
    return [pltpu.VMEM(shape, jnp.bfloat16) for shape in shapes]


def shape_of(dims, kind=jnp.bfloat16):
    return jax.ShapeDtypeStruct(dims, kind)


params = pltpu.CompilerParams(vmem_limit_bytes=VMEM_BYTES)


ANYWHERE = pl.BlockSpec(memory_space=pl.ANY)
DMAS = pltpu.SemaphoreType.DMA((40,))
SAVED = (
    (ALL_TOKENS, jnp.bfloat16),
    (ALL_TOKENS, jnp.bfloat16),
    (ALL_TOKENS, jnp.bfloat16),
    (ALL_TOKENS, jnp.bfloat16),
    ((BATCHES, WIDE, TOKENS), jnp.float32),
    (ALL_TOKENS, jnp.bfloat16),
    (ALL_TOKENS, jnp.float32),
    (ALL_TOKENS, jnp.bfloat16),
    (ALL_TOKENS, jnp.bfloat16),
    ((BATCHES, WIDE, STATES), jnp.float32),
    (ALL_TOKENS, jnp.bfloat16),
    (ALL_TOKENS, jnp.float32),
    (ALL_TOKENS, jnp.bfloat16),
    (HIDDEN, jnp.float32),
    (HIDDEN, jnp.float32),
    (HIDDEN, jnp.bfloat16),
)


def run_first(x, enc, self_add, cross_add, gains, weight):
    outs = [shape_of(ALL_TOKENS), shape_of(ALL_STATES), shape_of(ALL_STATES)]
    return pl.pallas_call(
        first_kernel,
        out_shape=outs,
        in_specs=in_vmem(5) + [pl.BlockSpec(memory_space=pl.ANY)],
        out_specs=in_vmem(len(outs)),
        scratch_shapes=[pltpu.VMEM(dims, kind) for dims, kind in SAVED]
        + held(*[FULL] * 8, GATED, GATED, DOWN)
        + [pltpu.SemaphoreType.DMA((40,))],
        compiler_params=params,
        name="first_forward",
    )(x, enc, self_add, cross_add, gains, weight)


def run_turn(x, ck, cv, self_add, cross_add, gains, cotangent, weight):
    saved = [shape_of(dims, kind) for dims, kind in SAVED]
    return pl.pallas_call(
        turn_kernel,
        out_shape=[shape_of(ALL_TOKENS)] * 2 + saved,
        in_specs=in_vmem(7) + [ANYWHERE],
        out_specs=in_vmem(2) + [ANYWHERE] * len(saved),
        scratch_shapes=[pltpu.VMEM(dims, kind) for dims, kind in SAVED]
        + held(ALL_TOKENS, ALL_TOKENS, ALL_STATES, ALL_STATES, *[ALL_TOKENS] * 4)
        + held(*[FULL] * 6, GATED, GATED, DOWN)
        + [DMAS, DMAS],
        compiler_params=params,
        name="forward_and_back",
    )(x, ck, cv, self_add, cross_add, gains, cotangent, weight)


HALF = (RING, RING, ROWS_OWN, ATT // 2)
RINGED = (RING, RING, ROWS_OWN, WIDE)
RINGED_WIDE = (RING, RING, ROWS_OWN, FF)
RINGED_TALL = (RING, RING, FF // PARTS // 2, WIDE)


def run_hidden(cotangent, gains, saved, weight):
    (ck, cv, n1, q, k, v, p, o, a2, n2, cq, cp, co, a3, n3, gate, up, hid) = saved
    return pl.pallas_call(
        hidden_kernel,
        out_shape=[
            shape_of(ALL_TOKENS, jnp.float32),
            shape_of((1, WIDE), jnp.float32),
            shape_of(HALF),
            shape_of(HALF),
        ],
        in_specs=in_vmem(7) + [ANYWHERE],
        out_specs=in_vmem(2) + [ANYWHERE, ANYWHERE],
        scratch_shapes=held(
            GATED, GATED, DOWN, RINGED_WIDE, RINGED_WIDE, RINGED_TALL, RINGED_TALL
        )
        + [DMAS, DMAS],
        compiler_params=params,
        name="hidden_backward",
    )(cotangent, a3, gains, gate, up, n3, hid, weight)


def run_cross(stream, gains, saved, weight):
    (ck, cv, n1, q, k, v, p, o, a2, n2, cq, cp, co, a3, n3, gate, up, hid) = saved
    return pl.pallas_call(
        cross_kernel,
        out_shape=[
            shape_of(ALL_TOKENS, jnp.float32),
            shape_of((1, WIDE), jnp.float32),
            shape_of(ALL_TOKENS),
            shape_of(ALL_TOKENS),
            shape_of(ALL_STATES),
            shape_of(ALL_STATES),
        ],
        in_specs=in_vmem(7) + [ANYWHERE],
        out_specs=in_vmem(6),
        scratch_shapes=held(FULL, FULL) + [DMAS],
        compiler_params=params,
        name="cross_backward",
    )(stream, gains, a2, cq, ck, cv, cp, weight)


def run_self(stream, x, gains, enc, saved, records, weight):
    (ck, cv, n1, q, k, v, p, o, a2, n2, cq, cp, co, a3, n3, gate, up, hid) = saved
    return pl.pallas_call(
        self_kernel,
        out_shape=[
            shape_of(ALL_TOKENS),
            shape_of((1, WIDE), jnp.float32),
            shape_of((WIDE, TOKENS), jnp.float32),
            shape_of(ALL_STATES),
            shape_of(HALF),
            shape_of(HALF),
        ],
        in_specs=in_vmem(16) + [ANYWHERE],
        out_specs=in_vmem(4) + [ANYWHERE, ANYWHERE],
        scratch_shapes=held(*[ALL_TOKENS] * 4, *[FULL] * 6, *[RINGED] * 8) + [DMAS, DMAS],
        compiler_params=params,
        name="self_backward",
    )(stream, x, gains, q, k, v, p, enc, n1, o, n2, co, *records, weight)


def pack_kernel(
    query_ref, kv_ref, out_ref, c_query_ref, c_kv_ref, c_out_ref, in_ref, ffn_ref, kept, given
):
    def attention(target):
        start = 0
        for ref in (query_ref, kv_ref, out_ref, c_query_ref, c_kv_ref, c_out_ref):
            if len(ref.shape) == 3:
                pair = ref[...].astype(jnp.float32)
                members = [low(pair[:, 0, :]), low(pair[:, 1, :])]
            else:
                members = [ref[...]]
            for member in members:
                target[:, start : start + WIDE] = member
                start += WIDE

    def hidden(target):
        pair = in_ref[...].astype(jnp.float32)
        target[:, :FF] = low(pair[:, 0, :])
        target[:, FF : 2 * FF] = low(pair[:, 1, :])
        for piece, block in DOWN_PIECES:
            lanes = pl.ds(2 * FF + GROUP * block, GROUP)
            target[pl.ds(16 * piece, 16), lanes] = ffn_ref[
                pl.ds(16 * block, 16), pl.ds(GROUP * piece, GROUP)
            ]

    @pl.when(core_is(0))
    def _():
        attention(kept)
        hidden(given)

    @pl.when(core_is(1))
    def _():
        hidden(kept)
        attention(given)


def run_pack(members):
    return pl.pallas_call(
        pack_kernel,
        out_shape=[shape_of((ROWS_OWN, ATT))] * 2,
        in_specs=in_vmem(8),
        out_specs=in_vmem(2),
        compiler_params=params,
        name="pack_weights",
    )(*members)


def add_kernel(left, right, total):
    total[...] = low(left[...].astype(jnp.float32) + right[...].astype(jnp.float32))


def add_halves(keep, received):
    dims = (WIDE, ATT // 2)
    spec = pl.BlockSpec((128, ATT // 2), lambda place: (place, 0))
    return pl.pallas_call(
        add_kernel,
        out_shape=shape_of(dims),
        grid=(6,),
        in_specs=[spec, spec],
        out_specs=spec,
        compiler_params=params,
        name="add_halves",
    )(keep.reshape(dims), received.reshape(dims))


def unpack_kernel(
    mine, theirs, query_ref, kv_ref, out_ref, c_query_ref, c_kv_ref, c_out_ref, in_ref, ffn_ref
):
    def write(first, second):
        def square_at(part, place):
            start = ATT // 2 + WIDE * place
            return part[:, start : start + WIDE].astype(jnp.float32)

        c_out_ref[...] = square_at(first, 0)
        c_query_ref[...] = square_at(first, 1)
        out_ref[...] = square_at(first, 2)
        query_ref[...] = square_at(first, 3)
        c_kv_ref[:, 0, :] = square_at(second, 0)
        c_kv_ref[:, 1, :] = square_at(second, 1)
        kv_ref[:, 0, :] = square_at(second, 2)
        kv_ref[:, 1, :] = square_at(second, 3)
        for index, part in enumerate((first, second)):
            in_ref[:, index, :] = part[:, :FF].astype(jnp.float32)
            for piece in range(GROUPS):
                for block in range(4):
                    rows = pl.ds(64 * index + 16 * block, 16)
                    taken = part[pl.ds(16 * piece, 16), pl.ds(FF + GROUP * block, GROUP)]
                    ffn_ref[rows, pl.ds(GROUP * piece, GROUP)] = taken.astype(jnp.float32)

    @pl.when(core_is(0))
    def _():
        write(mine, theirs)

    @pl.when(core_is(1))
    def _():
        write(theirs, mine)


def run_unpack(mine, theirs):
    wide = jnp.float32
    square_dims, pair_dims = (ROWS_OWN, WIDE), (ROWS_OWN, 2, WIDE)
    outs = [square_dims, pair_dims, square_dims, square_dims, pair_dims, square_dims]
    outs += [(ROWS_OWN, 2, FF), (FF // PARTS, WIDE)]
    return pl.pallas_call(
        unpack_kernel,
        out_shape=[shape_of(dims, wide) for dims in outs],
        in_specs=in_vmem(2),
        out_specs=in_vmem(8),
        compiler_params=params,
        name="unpack_gradients",
    )(mine, theirs)


def score_terms(table, dec_ids, enc_ids):
    positions = jnp.arange(TOKENS)
    by_distance = jnp.dot(table.astype(jnp.float32).T, bucket_onehot(TOKENS), precision=highest)
    bias = spread_distance(by_distance)
    allowed = (dec_ids[:, :, None] == dec_ids[:, None, :]) & (
        positions[None, :] <= positions[:, None]
    )
    self_add = jnp.where(allowed[:, None], bias[None], -jnp.inf)
    cross_add = jnp.where(dec_ids[:, :, None] == enc_ids[:, None, :], 0.0, -jnp.inf)
    return self_add.reshape(BATCHES, WIDE, TOKENS), cross_add


def shards(
    layer_in,
    cotangent,
    encoder,
    dec_segments,
    enc_segments,
    norm_gains,
    self_query,
    self_kv,
    self_out,
    rel_bias,
    cross_query,
    cross_kv,
    cross_out,
    ffn_in,
    ffn_out,
):
    core = lax.axis_index("section")
    part_index = lax.axis_index("fsdp")
    plane = lax.axis_index("rep")
    planes = lax.axis_size("rep")
    layer = lax.rem(plane, 2)
    first_core = core == 0
    at_home = core == layer

    def place(core_index, plane_index):
        return core_index * planes + plane_index

    def flip_core(value):
        return lax.ppermute(value, "section", [(0, 1), (1, 0)])

    def from_home(value):
        pairs = [(place(p % 2, p), place(1 - p % 2, p)) for p in range(planes)]
        return jnp.where(at_home, value, lax.ppermute(value, ("section", "rep"), pairs))

    def beside(value):
        return lax.ppermute(value, "rep", [(p, p ^ 1) for p in range(planes)])

    def rows_for_layer(value):
        pairs = [(place(p % 2, p), place(p % 2, p ^ 1)) for p in range(planes)]
        return jnp.where(at_home, value, lax.ppermute(value, ("section", "rep"), pairs))

    def rows_back(value):
        pairs = [(place(1 - p % 2, p), place(p % 2, p ^ 1)) for p in range(planes)]
        return jnp.where(at_home, value, lax.ppermute(value, ("section", "rep"), pairs))

    def between_layers(value, steps):
        pairs = [(p, p + steps) for p in range(planes) if p % 2 == (steps < 0)]
        return lax.ppermute(value, "rep", pairs)

    along_z = [[RING * x + z for z in range(RING)] for x in range(RING)]
    along_x = [[RING * x + z for x in range(RING)] for z in range(RING)]
    first_rings = along_z + [[PARTS + d for d in ring] for ring in along_x]
    second_rings = along_x + [[PARTS + d for d in ring] for ring in along_z]

    def scatter(value, rings):
        return lax.psum_scatter(
            value, ("section", "fsdp"), scatter_dimension=0, axis_index_groups=rings, tiled=True
        )

    kept, given_away = run_pack(
        [
            member[0]
            for member in (
                self_query,
                self_kv,
                self_out,
                cross_query,
                cross_kv,
                cross_out,
                ffn_in,
                ffn_out,
            )
        ]
    )
    half = jnp.where(at_home, kept, flip_core(given_away))
    weight = lax.all_gather(half, ("fsdp", "section"), axis=0, tiled=True)
    weight = weight.reshape(PARTS, 2, ROWS_OWN, ATT)
    small = jnp.zeros((8, 128), jnp.bfloat16)
    small = small.at[:3, :ROWS_OWN].set(norm_gains[0])
    small = small.at[3:5, :HEADS].set(rel_bias[0])
    small = lax.all_gather(from_home(small), "fsdp", axis=0, tiled=False)
    gains = small[:, :3, :ROWS_OWN].transpose(1, 0, 2).reshape(3, WIDE).astype(jnp.float32)
    table = small[:, 3:5, :HEADS].reshape(BUCKETS, HEADS)
    ids = jnp.concatenate([dec_segments[:, 0], enc_segments[:, 0]], axis=1)
    ids = rows_for_layer(ids)
    self_add, cross_add = score_terms(table, ids[:, :TOKENS], ids[:, TOKENS:])
    ends = jnp.stack([layer_in[:, 0].reshape(ALL_TOKENS), cotangent[:, 0].reshape(ALL_TOKENS)])
    ends = rows_for_layer(ends)
    rows_in, given = ends[0], ends[1]
    enc = rows_for_layer(encoder[:, 0].reshape(ALL_STATES))
    weight, rows_in, given, enc, self_add, cross_add, gains = lax.optimization_barrier(
        (weight, rows_in, given, enc, self_add, cross_add, gains)
    )
    first, ck, cv = run_first(rows_in, enc, self_add, cross_add, gains, weight)
    current = jnp.where(layer == 0, rows_in, between_layers(first, 1))
    result, grad_first, *saved = run_turn(
        current, ck, cv, self_add, cross_add, gains, given, weight
    )
    saved = [ck, cv] + saved
    incoming = jnp.where(layer == 1, given, between_layers(grad_first, -1))
    stream, gain_three, keep, send = run_hidden(incoming, gains, saved, weight)
    received = flip_core(send)
    stream, gain_two, *records = run_cross(stream, gains, saved, weight)
    wide_sum = add_halves(keep, received)
    wide_sum, stream = lax.optimization_barrier((wide_sum, stream))
    wide_part = scatter(wide_sum, first_rings)
    grad_input, gain_one, grad_scores, grad_enc, keep, send = run_self(
        stream, current, gains, enc, saved, records, weight
    )
    square_part = scatter(add_halves(keep, flip_core(send)), first_rings)
    grad_gains = jnp.concatenate([gain_one, gain_two, gain_three], axis=0)
    diagonal_sums = gather_distance(grad_scores.reshape(HEADS, TOKENS, TOKENS))
    grad_table = jnp.dot(bucket_onehot(TOKENS), diagonal_sums.T, precision=highest)
    little = jnp.zeros((8, WIDE), jnp.float32)
    little = little.at[:3].set(grad_gains)
    little = little.at[3, : BUCKETS * HEADS].set(grad_table.reshape(-1))
    for axis, bits in (("section", (1,)), ("fsdp", (1, 2, 4, 8)), ("rep", (2,))):
        for bit in bits:
            pairs = [(index, index ^ bit) for index in range(lax.axis_size(axis))]
            little = little + lax.ppermute(little, axis, pairs)
    little = jnp.where(at_home, little, beside(little))
    own_gains = lax.dynamic_slice(little, (0, part_index * ROWS_OWN), (3, ROWS_OWN))
    own_table = lax.dynamic_slice(little, (3, part_index * 2 * HEADS), (1, 2 * HEADS))
    outs = rows_back(jnp.stack([result, grad_input]))
    other_enc = beside(grad_enc)
    wide_part, square_part, own_gains, own_table, outs, other_enc = lax.optimization_barrier(
        (wide_part, square_part, own_gains, own_table, outs, other_enc)
    )
    partial = scatter(jnp.concatenate([wide_part, square_part], axis=1), second_rings)
    encoder_total = grad_enc.astype(jnp.float32) + other_enc.astype(jnp.float32)
    encoder_total = from_home(encoder_total)
    own_table = own_table.reshape(2, HEADS)
    results = (
        outs[0].reshape(1, BATCHES, 1, TOKENS, WIDE),
        outs[1].reshape(1, BATCHES, 1, TOKENS, WIDE),
        encoder_total.reshape(BATCHES, 1, STATES, WIDE),
        own_gains[None],
        own_table[None],
    )
    partial, results = lax.optimization_barrier((partial, results))
    up = [(p, (p + 1) % planes) for p in range(planes)]
    down = [(p, (p - 1) % planes) for p in range(planes)]
    across = [(p, (p + 2) % planes) for p in range(planes)]
    cut = ATT // 2
    outer = (plane == 0) | (plane == planes - 1)
    lower = plane < 2
    rising = lax.ppermute(jnp.where(outer, partial[:, :cut], partial[:, cut:]), "rep", up)
    falling = lax.ppermute(jnp.where(outer, partial[:, cut:], partial[:, :cut]), "rep", down)
    here = low(rising.astype(jnp.float32) + falling.astype(jnp.float32))
    below = lax.ppermute(here, "rep", up)
    above = lax.ppermute(here, "rep", down)
    beyond = lax.ppermute(here, "rep", across)
    own_layer = (jnp.where(outer, above, below), jnp.where(outer, below, above))
    other_layer = (jnp.where(lower, here, beyond), jnp.where(lower, beyond, here))
    pairs = list(zip(own_layer, other_layer))
    mine = jnp.concatenate([jnp.where(at_home, own, other) for own, other in pairs], axis=1)
    away = jnp.concatenate([jnp.where(at_home, other, own) for own, other in pairs], axis=1)
    query, kv, out, *others = [member[None] for member in run_unpack(mine, flip_core(away))]
    return (*results[:4], query, kv, out, results[4], *others)


def solution(mesh):
    return jax.shard_map(
        shards,
        mesh=mesh,
        in_specs=(
            P(None, ("fsdp", "rep"), None, None),
            P(None, ("fsdp", "rep"), None, None),
            P(None, ("fsdp", "rep"), None, None),
            P(None, ("fsdp", "rep"), None),
            P(None, ("fsdp", "rep"), None),
            P("section", None, "fsdp"),
            P("section", "fsdp", None),
            P("section", "fsdp", None, None),
            P("section", "fsdp", None),
            P("section", "fsdp", None),
            P("section", "fsdp", None),
            P("section", "fsdp", None, None),
            P("section", "fsdp", None),
            P("section", "fsdp", None, None),
            P("section", "fsdp", None),
        ),
        out_specs=(
            P("section", None, ("fsdp", "rep"), None, None),
            P("section", None, ("fsdp", "rep"), None, None),
            P(None, ("fsdp", "rep"), None, None),
            P("section", None, "fsdp"),
            P("section", "fsdp", None),
            P("section", "fsdp", None, None),
            P("section", "fsdp", None),
            P("section", "fsdp", None),
            P("section", "fsdp", None),
            P("section", "fsdp", None, None),
            P("section", "fsdp", None),
            P("section", "fsdp", None, None),
            P("section", "fsdp", None),
        ),
        check_vma=False,
    )
```

profile of v0, /device:TPU:1, one launch (start us, length us, event | category | flops | bytes accessed | tf_op | source)
XLA Modules:
  0.0 320.0 jit_solution(17661637337882096689)
XLA Ops:
  7.3 4.2 %pack_weights.1 = (bf16[48,6144]{1,0:T(8,128)(2,1)}, bf16[48,6144]{1,0:T(8,128)(2,1)}) custom-call(bf16[48,768]{1,0:T(8,128)(2,1)} %bitcast.93, bf16[48,2,768]{2,1,0:T(2,128)(2,1)} %bitcast.89, bf16[48,768]{1,0:T(8,128)(2,1)} %bitcast.94, bf16[48,768]{1,0:T(8,128)(2,1)} %bitcast.95, bf16[48,2,768]{2,1,0:T(2,128)(2,1)} %bitcast.90, bf16[48,768]{1,0:T(8,128)(2,1)} %bitcast.96, ...), custom_call_target="tpu_custom_call" | custom-call | tf_op jit(solution)/shard_map/pack_weights/pallas_call | solution.py:757
  11.5 1.4 collective-permute-start
  12.9 1.8 collective-permute-done
  14.7 0.9 broadcast_select_fusion.2
  15.8 1.3 collective-permute-start.3
  17.4 1.3 collective-permute-start.4
  18.7 0.8 pad_maximum_fusion.3
  19.5 1.3 collective-permute-start.1
  20.8 1.3 collective-permute-start.2
  22.1 21.1 %all-gather = bf16[128,128]{1,0:T(8,128)(2,1)S(1)} all-gather(bf16[8,128]{1,0:T(8,128)(2,1)S(1)} %broadcast_select_fusion.19), channel_id=2, replica_groups=mesh['section'=2,'fsdp'=16,'rep'=4] {'fsdp'}, dimensions={0}, use_global_device_ids=true | all-gather | bytes 34816 | tf_op jit(solution)/shard_map/all_gather | solution.py:926
  45.2 1.0 bitcast_select_fusion.self_add_ref
  46.1 0.7 compare_select_fusion.cross_add_ref
  46.9 1.0 broadcast_select_fusion.4
  47.9 0.8 slice_bitcast_fusion
  48.7 1.0 broadcast_select_fusion.1.enc_ref
  49.7 47.5 %all-gather.3.cloned.1.call-done = bf16[1536,6144]{1,0:T(8,128)(2,1)} async-done(((bf16[48,6144]{1,0:T(8,128)(2,1)}), bf16[1536,6144]{1,0:T(8,128)(2,1)}) %all-gather.3.cloned.1.call-update) | async-done | bytes 18874384 | tf_op jit(solution)/shard_map/all_gather | solution.py:921
  97.2 12.8 %first_forward.1 = (bf16[128,768]{1,0:T(8,128)(2,1)}, bf16[512,768]{1,0:T(8,128)(2,1)}, bf16[512,768]{1,0:T(8,128)(2,1)}) custom-call(bf16[128,768]{1,0:T(8,128)(2,1)} %get-tuple-element.132.x_ref, bf16[512,768]{1,0:T(8,128)(2,1)} %broadcast_select_fusion.1.enc_ref, f32[2,768,64]{2,1,0:T(8,128)} %bitcast_select_fusion.self_add_ref, ...), custom_call_target="tpu_custom_call" | custom-call | tf_op jit(solution)/shard_map/first_forward/pallas_call | solution.py:624
  110.0 3.7 %collective-permute-start.5 = (bf16[128,768]{1,0:T(8,128)(2,1)}, bf16[128,768]{1,0:T(8,128)(2,1)S(1)}, u32[]{:S(2)}, u32[]{:S(2)}) collective-permute-start(bf16[128,768]{1,0:T(8,128)(2,1)} %get-tuple-element.138), channel_id=1, source_target_pairs={{0,1},{2,3},{4,5},{6,7},{8,9},{10,11},{12,13},{14,15},{16,17},{18,... | collective-permute-start | bytes 589832 | tf_op jit(solution)/shard_map/ppermute | solution.py:893
  113.7 3.8 %collective-permute-done.5 = bf16[128,768]{1,0:T(8,128)(2,1)S(1)} collective-permute-done((bf16[128,768]{1,0:T(8,128)(2,1)}, bf16[128,768]{1,0:T(8,128)(2,1)S(1)}, u32[]{:S(2)}, u32[]{:S(2)}) %collective-permute-start.5) | collective-permute-done | bytes 196640 | tf_op jit(solution)/shard_map/ppermute | solution.py:893
  118.2 22.8 %forward_and_back.1 = (bf16[128,768]{1,0:T(8,128)(2,1)}, bf16[128,768]{1,0:T(8,128)(2,1)}, bf16[128,768]{1,0:T(8,128)(2,1)}, bf16[128,768]{1,0:T(8,128)(2,1)}, b...) custom-call(bf16[128,768]{1,0:T(8,128)(2,1)} %broadcast_select_fusio, ...), custom_call_target="tpu_custom_call" | custom-call | tf_op jit(solution)/shard_map/forward_and_back/pallas_call | solution.py:639
  141.0 1.3 collective-permute-start.6
  142.3 6.2 %collective-permute-done.6 = bf16[128,768]{1,0:T(8,128)(2,1)S(1)} collective-permute-done((bf16[128,768]{1,0:T(8,128)(2,1)}, bf16[128,768]{1,0:T(8,128)(2,1)S(1)}, u32[]{:S(2)}, u32[]{:S(2)}) %collective-permute-start.6) | collective-permute-done | bytes 196640 | tf_op jit(solution)/shard_map/ppermute | solution.py:893
  149.2 13.3 %hidden_backward.1 = (f32[128,768]{1,0:T(8,128)}, f32[1,768]{1,0:T(1,128)}, bf16[4,4,48,3072]{3,2,1,0:T(8,128)(2,1)}, bf16[4,4,48,3072]{3,2,1,0:T(8,128)(2,1)}) custom-call(bf16[128,768]{1,0:T(8,128)(2,1)} %broadcast_select_fusion.16.c_ref, f32[128,768]{1,0:T(8,128)} %get-tuple-element.142.a3_ref, f32[3,768]{1,0:T(4,128)} %reshape.217.gains_ref, ...), custom_call_target="tpu_custom_call" | custom-call | tf_op jit(solution)/shard_map/hidden_backward/pallas_call | solution.py:661
  162.5 2.1 collective-permute-start.7
  164.6 7.9 %cross_backward.1 = (f32[128,768]{1,0:T(8,128)}, f32[1,768]{1,0:T(1,128)}, bf16[128,768]{1,0:T(8,128)(2,1)}, bf16[128,768]{1,0:T(8,128)(2,1)}, bf16[512,768]{1,0:T(8,128)(2,1)}, /*index=5*/bf16[512,768]{1,0:T(8,128)(2,1)}) custom-call(f32[128,768]{1,0:T(8,128)} %get-tuple-element.149.stream_ref, f32[3,768]{1,0:T(4,128)} %reshape.217.gains_ref, ...), custom_call_target="tpu_custom_call" | custom-call | tf_op jit(solution)/shard_map/cross_backward/pallas_call | solution.py:682
  172.5 7.3 %add_halves.2 = bf16[768,3072]{1,0:T(8,128)(2,1)} custom-call(bf16[768,3072]{1,0:T(8,128)(2,1)} %bitcast.68, bf16[768,3072]{1,0:T(8,128)(2,1)} %bitcast.23.right), custom_call_target="tpu_custom_call" | custom-call | tf_op jit(solution)/shard_map/add_halves/pallas_call | solution.py:774
  180.1 13.4 %self_backward.1 = (bf16[128,768]{1,0:T(8,128)(2,1)}, f32[1,768]{1,0:T(1,128)}, f32[768,64]{1,0:T(8,128)}, bf16[512,768]{1,0:T(8,128)(2,1)}, bf16[4,4,48,3072]{3...) custom-call(f32[128,768]{1,0:T(8,128)} %get-tuple-element.155.stream_ref, ...), custom_call_target="tpu_custom_call" | custom-call | tf_op jit(solution)/shard_map/self_backward/pallas_call | solution.py:702
  193.9 7.9 %collective-permute-done.8 = bf16[4,4,48,3072]{3,2,1,0:T(8,128)(2,1)} collective-permute-done((bf16[4,4,48,3072]{3,2,1,0:T(8,128)(2,1)}, bf16[4,4,48,3072]{3,2,1,0:T(8,128)(2,1)}, u32[]{:S(2)}, u32[]{:S(2)}) %collective-permute-start.8) | collective-permute-done | bytes 4718624 | tf_op jit(solution)/shard_map/ppermute | solution.py:874
  201.8 7.3 %add_halves.3 = bf16[768,3072]{1,0:T(8,128)(2,1)} custom-call(bf16[768,3072]{1,0:T(8,128)(2,1)} %bitcast.67, bf16[768,3072]{1,0:T(8,128)(2,1)} %bitcast.25.right), custom_call_target="tpu_custom_call" | custom-call | tf_op jit(solution)/shard_map/add_halves/pallas_call | solution.py:774
  209.2 0.9 copy-done.9
  210.8 0.7 reshape.214
  212.8 0.8 collective-permute-done.9
  214.2 2.2 collective-permute-done.10
  216.3 2.1 collective-permute-start.11
  218.5 2.0 collective-permute-done.11
  220.5 1.2 collective-permute-start.12
  221.7 1.5 collective-permute-done.12
  223.2 2.7 collective-permute-start.13
  225.9 1.8 collective-permute-done.13
  227.6 2.4 collective-permute-start.14
  230.1 2.1 collective-permute-done.14
  232.2 10.1 %collective-permute-start.16 = (bf16[2,128,768]{2,1,0:T(8,128)(2,1)S(1)}, bf16[2,128,768]{2,1,0:T(8,128)(2,1)S(1)}, u32[]{:S(2)}, u32[]{:S(2)}) collective-permute-start(bf16[2,128,768]{2,1,0:T(8,128)(2,1)S(1)} %pad_maximum_fusion.4), channel_id=1, source_target_pairs={{64,1},{1,64},{66,3},{3,66},{68,5},{5,68},{70,7},{7,70},{72,9},{9,... | collective-permute-start | bytes 1179656 | tf_op jit(solution)/shard_map/ppermute | solution.py:889
  242.3 2.4 collective-permute-done.15
  244.9 9.4 %collective-permute-done.16 = bf16[2,128,768]{2,1,0:T(8,128)(2,1)S(1)} collective-permute-done((bf16[2,128,768]{2,1,0:T(8,128)(2,1)S(1)}, bf16[2,128,768]{2,1,0:T(8,128)(2,1)S(1)}, u32[]{:S(2)}, u32[]{:S(2)}) %collective-permute-start.16) | collective-permute-done | bytes 393248 | tf_op jit(solution)/shard_map/ppermute | solution.py:889
  254.5 3.2 %pad_maximum_fusion = bf16[192,6144]{1,0:T(8,128)(2,1)} fusion(bf16[192,3072]{1,0:T(8,128)(2,1)} %reduce-scatter.6.cloned.1.call-done, bf16[192,3072]{1,0:T(8,128)(2,1)} %reduce-scatter.4.cloned.1.call-done), kind=kLoop, calls=%fused_computation | loop fusion | flops 4718592 | bytes 4718592 | tf_op jit(solution)/shard_map/concatenate | solution.py:974
  257.7 1.3 convert_add_fusion
  259.0 1.3 collective-permute-start.18
  262.1 0.8 fusion.2
  262.9 1.6 collective-permute-done.18
  264.5 1.3 broadcast_select_fusion
  265.9 13.2 %reduce-scatter.8.cloned.1.call-done = bf16[48,6144]{1,0:T(8,128)(2,1)} async-done(((bf16[192,6144]{1,0:T(8,128)(2,1)}), bf16[48,6144]{1,0:T(8,128)(2,1)}) %reduce-scatter.8.cloned.1.call-update) | async-done | bytes 589840 | tf_op jit(solution)/shard_map/reduce_scatter | solution.py:901
  279.0 1.1 broadcast_select_fusion.10
  280.1 1.3 collective-permute-start.19
  281.4 1.5 collective-permute-start.20
  282.9 5.2 %collective-permute-done.19 = bf16[48,3072]{1,0:T(8,128)(2,1)S(1)} collective-permute-done((bf16[48,3072]{1,0:T(8,128)(2,1)S(1)}, bf16[48,3072]{1,0:T(8,128)(2,1)S(1)}, u32[]{:S(2)}, u32[]{:S(2)}) %collective-permute-start.19) | collective-permute-done | bytes 294944 | tf_op jit(solution)/shard_map/ppermute | solution.py:992
  288.1 2.5 collective-permute-start.21
  290.6 1.3 collective-permute-start.23
  292.4 1.8 collective-permute-done.21
  294.3 6.8 %collective-permute-done.22 = bf16[48,3072]{1,0:T(8,128)(2,1)S(1)} collective-permute-done((bf16[48,3072]{1,0:T(8,128)(2,1)S(1)}, bf16[48,3072]{1,0:T(8,128)(2,1)S(1)}, u32[]{:S(2)}, u32[]{:S(2)}) %collective-permute-start.22) | collective-permute-done | bytes 294944 | tf_op jit(solution)/shard_map/ppermute | solution.py:995
  301.8 6.0 %collective-permute-start.24 = (bf16[48,6144]{1,0:T(8,128)(2,1)S(1)}, bf16[48,6144]{1,0:T(8,128)(2,1)S(1)}, u32[]{:S(2)}, u32[]{:S(2)}) collective-permute-start(bf16[48,6144]{1,0:T(8,128)(2,1)S(1)} %pad_maximum_fusion.2), channel_id=1, source_target_pairs={{0,64},{64,0},{1,65},{65,1},{2,66},{66,2},{3,67},{67,3},{4,68},{68... | collective-permute-start | bytes 1769480 | tf_op jit(solution)/shard_map/ppermute | solution.py:874
  307.8 0.9 pad_maximum_fusion.1.mine
  308.6 0.8 collective-permute-done.24.theirs
  309.4 0.8 copy-done.8
  310.2 3.0 unpack_gradients.1
  (109 shorter events, 10.4 us)
Async XLA Ops:
  7.2 90.0 %all-gather.3.cloned.1.call-start = ((), (), s32[]{:S(2)}) async-start(), calls=%async_computation.3 | async-start | bytes 19464192 | tf_op jit(solution)/shard_map/all_gather | solution.py:921
  7.2 8.5 %copy-start.15 = (s32[2,1,256]{2,1,0:T(1,128)S(1)}, s32[2,1,256]{2,1,0:T(1,128)}, u32[]{:S(2)}) copy-start(s32[2,1,256]{2,1,0:T(1,128)} %param.29) | copy-start | bytes 6148
  7.2 8.5 %copy-start.11 = (s32[2,1,64]{2,1,0:T(1,128)S(1)}, s32[2,1,64]{2,1,0:T(1,128)}, u32[]{:S(2)}) copy-start(s32[2,1,64]{2,1,0:T(1,128)} %param.28) | copy-start | bytes 1540
  7.2 9.8 %copy-start.16 = (bf16[1,3,48]{2,1,0:T(4,128)(2,1)S(1)}, bf16[1,3,48]{2,1,0:T(4,128)(2,1)}, u32[]{:S(2)}) copy-start(bf16[1,3,48]{2,1,0:T(4,128)(2,1)} %param.30) | copy-start | bytes 868
  7.3 9.8 %copy-start.17 = (bf16[1,2,12]{2,1,0:T(2,128)(2,1)S(1)}, bf16[1,2,12]{2,1,0:T(2,128)(2,1)}, u32[]{:S(2)}) copy-start(bf16[1,2,12]{2,1,0:T(2,128)(2,1)} %param.34) | copy-start | bytes 148
  7.3 11.4 %copy-start.4 = (bf16[2,1,64,768]{3,2,1,0:T(8,128)(2,1)S(1)}, bf16[2,1,64,768]{3,2,1,0:T(8,128)(2,1)}, u32[]{:S(2)}) copy-start(bf16[2,1,64,768]{3,2,1,0:T(8,128)(2,1)} %param.26) | copy-start | bytes 589828
  7.3 11.4 %copy-start.5 = (bf16[2,1,64,768]{3,2,1,0:T(8,128)(2,1)S(1)}, bf16[2,1,64,768]{3,2,1,0:T(8,128)(2,1)}, u32[]{:S(2)}) copy-start(bf16[2,1,64,768]{3,2,1,0:T(8,128)(2,1)} %param.25) | copy-start | bytes 589828
  11.5 3.3 %collective-permute-start = (bf16[48,6144]{1,0:T(8,128)(2,1)}, bf16[48,6144]{1,0:T(8,128)(2,1)S(1)}, u32[]{:S(2)}, u32[]{:S(2)}) collective-permute-start(bf16[48,6144]{1,0:T(8,128)(2,1)} %get-tuple-element.130), channel_id=1, source_target_pairs={{0,64},{64,0},{1,65},{65,1},{2,66},{66,2},{3,67},{67,3},{4,68},{68... | collective-permute-start | bytes 1769480 | tf_op jit(solution)/shard_map/ppermute | solution.py:874
  14.7 6.1 %copy-start.3 = (bf16[2,1,256,768]{3,2,1,0:T(8,128)(2,1)S(1)}, bf16[2,1,256,768]{3,2,1,0:T(8,128)(2,1)}, u32[]{:S(2)}) copy-start(bf16[2,1,256,768]{3,2,1,0:T(8,128)(2,1)} %param.27) | copy-start | bytes 2359300
  14.7 28.6 %copy-start.10 = (f32[32,64]{1,0:T(8,128)S(1)}, f32[32,64]{1,0:T(8,128)}, u32[]{:S(2)}) copy-start(f32[32,64]{1,0:T(8,128)} %constant.143.clone) | copy-start | bytes 24580
  15.6 238.8 %reduce-scatter.4.cloned.1.call-start = ((), (), s32[]{:S(2)}) async-start(), calls=%async_computation.4 | async-start | bytes 5898240 | tf_op jit(solution)/shard_map/reduce_scatter | solution.py:901
  15.8 29.2 %collective-permute-start.3 = (s32[2,320]{1,0:T(2,128)S(1)}, s32[2,320]{1,0:T(2,128)S(1)}, u32[]{:S(2)}, u32[]{:S(2)}) collective-permute-start(s32[2,320]{1,0:T(2,128)S(1)} %pad_add_fusion), channel_id=1, source_target_pairs={{0,1},{65,64},{2,3},{67,66},{4,5},{69,68},{6,7},{71,70},{8,9},{73,... | collective-permute-start | bytes 7688 | tf_op jit(solution)/shard_map/ppermute | solution.py:885
  17.4 4.7 %collective-permute-start.4 = (bf16[8,128]{1,0:T(8,128)(2,1)S(1)}, bf16[8,128]{1,0:T(8,128)(2,1)S(1)}, u32[]{:S(2)}, u32[]{:S(2)}) collective-permute-start(bf16[8,128]{1,0:T(8,128)(2,1)S(1)} %scatter.15), channel_id=1, source_target_pairs={{0,64},{65,1},{2,66},{67,3},{4,68},{69,5},{6,70},{71,7},{8,72},{73... | collective-permute-start | bytes 6152 | tf_op jit(solution)/shard_map/ppermute | solution.py:878
  19.5 27.4 %collective-permute-start.1 = (bf16[2,128,768]{2,1,0:T(8,128)(2,1)}, bf16[2,128,768]{2,1,0:T(8,128)(2,1)}, u32[]{:S(2)}, u32[]{:S(2)}) collective-permute-start(bf16[2,128,768]{2,1,0:T(8,128)(2,1)} %pad_maximum_fusion.3), channel_id=1, source_target_pairs={{0,1},{65,64},{2,3},{67,66},{4,5},{69,68},{6,7},{71,70},{8,9},{73,... | collective-permute-start | bytes 1179656 | tf_op jit(solution)/shard_map/ppermute | solution.py:885
  20.8 27.9 %collective-permute-start.2 = (bf16[512,768]{1,0:T(8,128)(2,1)S(1)}, bf16[512,768]{1,0:T(8,128)(2,1)S(1)}, u32[]{:S(2)}, u32[]{:S(2)}) collective-permute-start(bf16[512,768]{1,0:T(8,128)(2,1)S(1)} %bitcast.75), channel_id=1, source_target_pairs={{0,1},{65,64},{2,3},{67,66},{4,5},{69,68},{6,7},{71,70},{8,9},{73,... | collective-permute-start | bytes 2359304 | tf_op jit(solution)/shard_map/ppermute | solution.py:885
  97.2 20.2 %copy-start.2 = (bf16[128,768]{1,0:T(8,128)(2,1)S(1)}, bf16[128,768]{1,0:T(8,128)(2,1)}, u32[]{:S(2)}) copy-start(bf16[128,768]{1,0:T(8,128)(2,1)} %get-tuple-element.132.x_ref) | copy-start | bytes 589828
  110.0 7.5 %collective-permute-start.5 = (bf16[128,768]{1,0:T(8,128)(2,1)}, bf16[128,768]{1,0:T(8,128)(2,1)S(1)}, u32[]{:S(2)}, u32[]{:S(2)}) collective-permute-start(bf16[128,768]{1,0:T(8,128)(2,1)} %get-tuple-element.138), channel_id=1, source_target_pairs={{0,1},{2,3},{4,5},{6,7},{8,9},{10,11},{12,13},{14,15},{16,17},{18,... | collective-permute-start | bytes 589832 | tf_op jit(solution)/shard_map/ppermute | solution.py:893
  118.2 30.3 %copy-start.1 = (bf16[128,768]{1,0:T(8,128)(2,1)S(1)}, bf16[128,768]{1,0:T(8,128)(2,1)}, u32[]{:S(2)}) copy-start(bf16[128,768]{1,0:T(8,128)(2,1)} %get-tuple-element.131.c_ref) | copy-start | bytes 589828
  141.0 7.5 %collective-permute-start.6 = (bf16[128,768]{1,0:T(8,128)(2,1)}, bf16[128,768]{1,0:T(8,128)(2,1)S(1)}, u32[]{:S(2)}, u32[]{:S(2)}) collective-permute-start(bf16[128,768]{1,0:T(8,128)(2,1)} %get-tuple-element.141), channel_id=1, source_target_pairs={{1,0},{3,2},{5,4},{7,6},{9,8},{11,10},{13,12},{15,14},{17,16},{19,... | collective-permute-start | bytes 589832 | tf_op jit(solution)/shard_map/ppermute | solution.py:893
  162.5 10.0 %collective-permute-start.7 = (bf16[4,4,48,3072]{3,2,1,0:T(8,128)(2,1)}, bf16[4,4,48,3072]{3,2,1,0:T(8,128)(2,1)}, u32[]{:S(2)}, u32[]{:S(2)}) collective-permute-start(bf16[4,4,48,3072]{3,2,1,0:T(8,128)(2,1)} %get-tuple-element.148), channel_id=1, source_target_pairs={{0,64},{64,0},{1,65},{65,1},{2,66},{66,2},{3,67},{67,3},{4,68},{68... | collective-permute-start | bytes 14155784 | tf_op jit(solution)/shard_map/ppermute | solution.py:874
  179.8 74.7 %reduce-scatter.6.cloned.1.call-start = ((), (), s32[]{:S(2)}) async-start(), calls=%async_computation.5 | async-start | bytes 5898240 | tf_op jit(solution)/shard_map/reduce_scatter | solution.py:901
  193.5 8.3 %collective-permute-start.8 = (bf16[4,4,48,3072]{3,2,1,0:T(8,128)(2,1)}, bf16[4,4,48,3072]{3,2,1,0:T(8,128)(2,1)}, u32[]{:S(2)}, u32[]{:S(2)}) collective-permute-start(bf16[4,4,48,3072]{3,2,1,0:T(8,128)(2,1)} %get-tuple-element.169), channel_id=1, source_target_pairs={{0,64},{64,0},{1,65},{65,1},{2,66},{66,2},{3,67},{67,3},{4,68},{68... | collective-permute-start | bytes 14155784 | tf_op jit(solution)/shard_map/ppermute | solution.py:874
  209.2 1.0 copy-start.9
  209.2 69.9 %reduce-scatter.8.cloned.1.call-start = ((), (), s32[]{:S(2)}) async-start(), calls=%async_computation.6 | async-start | bytes 2949120 | tf_op jit(solution)/shard_map/reduce_scatter | solution.py:901
  210.4 1.5 copy-start.12
  210.4 1.5 copy-start.13
  210.4 1.5 copy-start.14
  210.5 19.6 %copy-start = (bf16[512,768]{1,0:T(8,128)(2,1)S(1)}, bf16[512,768]{1,0:T(8,128)(2,1)}, u32[]{:S(2)}) copy-start(bf16[512,768]{1,0:T(8,128)(2,1)} %get-tuple-element.176) | copy-start | bytes 2359300
  210.5 21.7 %copy-start.6 = (bf16[128,768]{1,0:T(8,128)(2,1)S(1)}, bf16[128,768]{1,0:T(8,128)(2,1)}, u32[]{:S(2)}) copy-start(bf16[128,768]{1,0:T(8,128)(2,1)} %get-tuple-element.174) | copy-start | bytes 589828
  210.5 21.7 %copy-start.7 = (bf16[128,768]{1,0:T(8,128)(2,1)S(1)}, bf16[128,768]{1,0:T(8,128)(2,1)}, u32[]{:S(2)}) copy-start(bf16[128,768]{1,0:T(8,128)(2,1)} %get-tuple-element.175) | copy-start | bytes 589828
  212.3 1.4 collective-permute-start.9
  213.6 2.7 collective-permute-start.10
  216.3 4.2 %collective-permute-start.11 = (f32[8,768]{1,0:T(8,128)S(1)}, f32[8,768]{1,0:T(8,128)S(1)}, u32[]{:S(2)}, u32[]{:S(2)}) collective-permute-start(f32[8,768]{1,0:T(8,128)S(1)} %add.55), channel_id=1, source_target_pairs={{0,8},{4,12},{8,0},{12,4},{16,24},{20,28},{24,16},{28,20},{32,40},... | collective-permute-start | bytes 73736 | tf_op jit(solution)/shard_map/ppermute | solution.py:965
  220.5 2.7 collective-permute-start.12
  223.2 4.4 %collective-permute-start.13 = (f32[8,768]{1,0:T(8,128)S(1)}, f32[8,768]{1,0:T(8,128)S(1)}, u32[]{:S(2)}, u32[]{:S(2)}) collective-permute-start(f32[8,768]{1,0:T(8,128)S(1)} %add.57), channel_id=1, source_target_pairs={{0,32},{4,36},{8,40},{12,44},{16,48},{20,52},{24,56},{28,60},{32,0... | collective-permute-start | bytes 73736 | tf_op jit(solution)/shard_map/ppermute | solution.py:965
  227.6 4.5 %collective-permute-start.14 = (f32[8,768]{1,0:T(8,128)S(1)}, f32[8,768]{1,0:T(8,128)S(1)}, u32[]{:S(2)}, u32[]{:S(2)}) collective-permute-start(f32[8,768]{1,0:T(8,128)S(1)} %add.58), channel_id=1, source_target_pairs={{0,2},{1,3},{2,0},{3,1},{4,6},{5,7},{6,4},{7,5},{8,10},{9,11},{10,... | collective-permute-start | bytes 73736 | tf_op jit(solution)/shard_map/ppermute | solution.py:965
  230.1 24.3 %collective-permute-start.17 = (bf16[512,768]{1,0:T(8,128)(2,1)S(1)}, bf16[512,768]{1,0:T(8,128)(2,1)S(1)}, u32[]{:S(2)}, u32[]{:S(2)}) collective-permute-start(bf16[512,768]{1,0:T(8,128)(2,1)S(1)} %copy-done), channel_id=1, source_target_pairs={{0,1},{1,0},{2,3},{3,2},{4,5},{5,4},{6,7},{7,6},{8,9},{9,8},{10,11... | collective-permute-start | bytes 2359304 | tf_op jit(solution)/shard_map/ppermute | solution.py:881
  232.1 12.6 %collective-permute-start.15 = (f32[8,768]{1,0:T(8,128)S(1)}, f32[8,768]{1,0:T(8,128)S(1)}, u32[]{:S(2)}, u32[]{:S(2)}) collective-permute-start(f32[8,768]{1,0:T(8,128)S(1)} %add.59), channel_id=1, source_target_pairs={{0,1},{1,0},{2,3},{3,2},{4,5},{5,4},{6,7},{7,6},{8,9},{9,8},{10,11... | collective-permute-start | bytes 73736 | tf_op jit(solution)/shard_map/ppermute | solution.py:881
  232.2 22.1 %collective-permute-start.16 = (bf16[2,128,768]{2,1,0:T(8,128)(2,1)S(1)}, bf16[2,128,768]{2,1,0:T(8,128)(2,1)S(1)}, u32[]{:S(2)}, u32[]{:S(2)}) collective-permute-start(bf16[2,128,768]{2,1,0:T(8,128)(2,1)S(1)} %pad_maximum_fusion.4), channel_id=1, source_target_pairs={{64,1},{1,64},{66,3},{3,66},{68,5},{5,68},{70,7},{7,70},{72,9},{9,... | collective-permute-start | bytes 1179656 | tf_op jit(solution)/shard_map/ppermute | solution.py:889
  259.0 5.5 %collective-permute-start.18 = (f32[512,768]{1,0:T(8,128)}, f32[512,768]{1,0:T(8,128)S(1)}, u32[]{:S(2)}, u32[]{:S(2)}) collective-permute-start(f32[512,768]{1,0:T(8,128)} %convert_add_fusion), channel_id=1, source_target_pairs={{0,64},{65,1},{2,66},{67,3},{4,68},{69,5},{6,70},{71,7},{8,72},{73... | collective-permute-start | bytes 4718600 | tf_op jit(solution)/shard_map/ppermute | solution.py:878
  280.1 7.9 %collective-permute-start.19 = (bf16[48,3072]{1,0:T(8,128)(2,1)S(1)}, bf16[48,3072]{1,0:T(8,128)(2,1)S(1)}, u32[]{:S(2)}, u32[]{:S(2)}) collective-permute-start(bf16[48,3072]{1,0:T(8,128)(2,1)S(1)} %get-tuple-element.227), channel_id=1, source_target_pairs={{0,1},{1,2},{2,3},{3,0},{4,5},{5,6},{6,7},{7,4},{8,9},{9,10},{10,1... | collective-permute-start | bytes 884744 | tf_op jit(solution)/shard_map/ppermute | solution.py:992
  281.4 6.6 %collective-permute-start.20 = (bf16[48,3072]{1,0:T(8,128)(2,1)S(1)}, bf16[48,3072]{1,0:T(8,128)(2,1)S(1)}, u32[]{:S(2)}, u32[]{:S(2)}) collective-permute-start(bf16[48,3072]{1,0:T(8,128)(2,1)S(1)} %get-tuple-element.228), channel_id=1, source_target_pairs={{0,3},{1,0},{2,1},{3,2},{4,7},{5,4},{6,5},{7,6},{8,11},{9,8},{10,9... | collective-permute-start | bytes 884744 | tf_op jit(solution)/shard_map/ppermute | solution.py:993
  288.1 6.1 %collective-permute-start.21 = (bf16[48,3072]{1,0:T(8,128)(2,1)S(1)}, bf16[48,3072]{1,0:T(8,128)(2,1)S(1)}, u32[]{:S(2)}, u32[]{:S(2)}) collective-permute-start(bf16[48,3072]{1,0:T(8,128)(2,1)S(1)} %add_convert_fusion), channel_id=1, source_target_pairs={{0,3},{1,0},{2,1},{3,2},{4,7},{5,4},{6,5},{7,6},{8,11},{9,8},{10,9... | collective-permute-start | bytes 884744 | tf_op jit(solution)/shard_map/ppermute | solution.py:996
  290.6 10.5 %collective-permute-start.22 = (bf16[48,3072]{1,0:T(8,128)(2,1)S(1)}, bf16[48,3072]{1,0:T(8,128)(2,1)S(1)}, u32[]{:S(2)}, u32[]{:S(2)}) collective-permute-start(bf16[48,3072]{1,0:T(8,128)(2,1)S(1)} %add_convert_fusion), channel_id=1, source_target_pairs={{0,1},{1,2},{2,3},{3,0},{4,5},{5,6},{6,7},{7,4},{8,9},{9,10},{10,1... | collective-permute-start | bytes 884744 | tf_op jit(solution)/shard_map/ppermute | solution.py:995
  290.6 11.0 %collective-permute-start.23 = (bf16[48,3072]{1,0:T(8,128)(2,1)S(1)}, bf16[48,3072]{1,0:T(8,128)(2,1)S(1)}, u32[]{:S(2)}, u32[]{:S(2)}) collective-permute-start(bf16[48,3072]{1,0:T(8,128)(2,1)S(1)} %add_convert_fusion), channel_id=1, source_target_pairs={{0,2},{1,3},{2,0},{3,1},{4,6},{5,7},{6,4},{7,5},{8,10},{9,11},{10,... | collective-permute-start | bytes 884744 | tf_op jit(solution)/shard_map/ppermute | solution.py:997
  301.8 7.6 %collective-permute-start.24 = (bf16[48,6144]{1,0:T(8,128)(2,1)S(1)}, bf16[48,6144]{1,0:T(8,128)(2,1)S(1)}, u32[]{:S(2)}, u32[]{:S(2)}) collective-permute-start(bf16[48,6144]{1,0:T(8,128)(2,1)S(1)} %pad_maximum_fusion.2), channel_id=1, source_target_pairs={{0,64},{64,0},{1,65},{65,1},{2,66},{66,2},{3,67},{67,3},{4,68},{68... | collective-permute-start | bytes 1769480 | tf_op jit(solution)/shard_map/ppermute | solution.py:874
  309.4 0.8 copy-start.8
Sparse Core Ops, SparseCore 0:
  15.8 81.4 all-gather.2
  179.9 31.1 reduce-scatter.3
  213.5 32.8 reduce-scatter.5
  257.9 21.1 reduce-scatter.7
where the time goes:
time: 325 us; the launch traced here: 320 us
  waiting for transfers between devices  119 us (37%)
  Pallas kernels  91.9 us (28%)
  starting transfers between devices  47.9 us (15%)
  blocking collectives  21.1 us (6%)
  other arithmetic  16 us (5%)
  between operations  14.7 us (5%)
  local copies, waits for them, and re-layouts  8.69 us (3%)
    all_gather x1, waiting for transfers between devices, shards(): weight = lax.all_gather(half, ('fsdp', 'section'), axis=0, tiled=True)  47.5 us
    pallas_call x1, Pallas kernels, run_turn(): pl.pallas_call(turn_kernel, out_shape=[shape_of(ALL_TOKENS)] * 2 + saved,...  22.8 us
    all_gather x1, blocking collectives, shards(): small = lax.all_gather(from_home(small), 'fsdp', axis=0, tiled=False)  21.1 us
    pallas_call x2, Pallas kernels, add_halves(): pl.pallas_call(add_kernel, out_shape=shape_of(dims), grid=(6,), in_specs=...  14.6 us
    pallas_call x1, Pallas kernels, run_self(): pl.pallas_call(self_kernel, out_shape=[shape_of(ALL_TOKENS), shape_of((1,...  13.4 us
    pallas_call x1, Pallas kernels, run_hidden(): pl.pallas_call(hidden_kernel, out_shape=[shape_of(ALL_TOKENS, jnp.float32...  13.3 us
    reduce_scatter x3, waiting for transfers between devices, scatter(): lax.psum_scatter(value, ('section', 'fsdp'), scatter_dimension=0, axis_in...  13.2 us
    pallas_call x1, Pallas kernels, run_first(): pl.pallas_call(first_kernel, out_shape=outs, in_specs=in_vmem(5) + [pl.Bl...  12.8 us
  transfers between devices with their start and end apart: 29, of which 20 were waited for; matrix products, arithmetic and copies ran while one was open for 5% of the time, Pallas kernels for 9%

commit v1 on v0

--- a/solution.py
+++ b/solution.py
@@ -770,11 +770,11 @@
 
 def add_halves(keep, received):
     dims = (WIDE, ATT // 2)
-    spec = pl.BlockSpec((128, ATT // 2), lambda place: (place, 0))
+    spec = pl.BlockSpec((64, ATT // 2), lambda place: (place, 0))
     return pl.pallas_call(
         add_kernel,
         out_shape=shape_of(dims),
-        grid=(6,),
+        grid=(12,),
         in_specs=[spec, spec],
         out_specs=spec,
         compiler_params=params,
@@ -825,7 +825,7 @@
         out_shape=[shape_of(dims, wide) for dims in outs],
         in_specs=in_vmem(2),
         out_specs=in_vmem(8),
-        compiler_params=params,
+        compiler_params=pltpu.CompilerParams(vmem_limit_bytes=10 * 1024 * 1024),
         name="unpack_gradients",
     )(mine, theirs)
 
@@ -880,6 +880,10 @@
     def beside(value):
         return lax.ppermute(value, "rep", [(p, p ^ 1) for p in range(planes)])
 
+    def to_home(value):
+        pairs = [(place(1 - p % 2, p), place(1 - p % 2, p ^ 1)) for p in range(planes)]
+        return lax.ppermute(value, ("section", "rep"), pairs)
+
     def rows_for_layer(value):
         pairs = [(place(p % 2, p), place(p % 2, p ^ 1)) for p in range(planes)]
         return jnp.where(at_home, value, lax.ppermute(value, ("section", "rep"), pairs))
@@ -959,19 +963,24 @@
     little = jnp.zeros((8, WIDE), jnp.float32)
     little = little.at[:3].set(grad_gains)
     little = little.at[3, : BUCKETS * HEADS].set(grad_table.reshape(-1))
-    for axis, bits in (("section", (1,)), ("fsdp", (1, 2, 4, 8)), ("rep", (2,))):
+
+    def add_pairs(value, axis, bits):
         for bit in bits:
             pairs = [(index, index ^ bit) for index in range(lax.axis_size(axis))]
-            little = little + lax.ppermute(little, axis, pairs)
+            value = value + lax.ppermute(value, axis, pairs)
+        return value
+
+    little = add_pairs(add_pairs(little, "section", (1,)), "fsdp", (1, 2, 4, 8))
+    outs = rows_back(jnp.stack([result, grad_input]))
+    wide_part, square_part, little, outs, grad_enc = lax.optimization_barrier(
+        (wide_part, square_part, little, outs, grad_enc)
+    )
+    partial = scatter(jnp.concatenate([wide_part, square_part], axis=1), second_rings)
+    other_enc = to_home(grad_enc)
+    little = add_pairs(little, "rep", (2,))
     little = jnp.where(at_home, little, beside(little))
     own_gains = lax.dynamic_slice(little, (0, part_index * ROWS_OWN), (3, ROWS_OWN))
     own_table = lax.dynamic_slice(little, (3, part_index * 2 * HEADS), (1, 2 * HEADS))
-    outs = rows_back(jnp.stack([result, grad_input]))
-    other_enc = beside(grad_enc)
-    wide_part, square_part, own_gains, own_table, outs, other_enc = lax.optimization_barrier(
-        (wide_part, square_part, own_gains, own_table, outs, other_enc)
-    )
-    partial = scatter(jnp.concatenate([wide_part, square_part], axis=1), second_rings)
     encoder_total = grad_enc.astype(jnp.float32) + other_enc.astype(jnp.float32)
     encoder_total = from_home(encoder_total)
     own_table = own_table.reshape(2, HEADS)

time: 325 us -> 324 us (level)
  Pallas kernels: 91.9 us -> 95.7 us
    ppermute x6 -> x7, waiting for transfers between devices: 10.3 us -> 20.3 us  [the longest x6 11.4 us: add_pairs(): value = value + lax.ppermute(value, axis, pairs)]
    ppermute x1, waiting for transfers between devices: 9.43 us -> 0.01 us  [rows_back(): lax.ppermute(value, ('section', 'rep'), pairs)]
    ppermute x1, starting transfers between devices: 10.1 us -> 1.92 us  [rows_back(): lax.ppermute(value, ('section', 'rep'), pairs)]
    pallas_call x2, Pallas kernels: 14.6 us -> 19.6 us  [add_halves(): pl.pallas_call(add_kernel, out_shape=shape_of(dims), grid=(12,), in_specs...]
    ppermute x6 -> x7, starting transfers between devices: 9.5 us -> 12.5 us  [the longest x6 9.33 us: add_pairs(): value = value + lax.ppermute(value, axis, pairs)]
  transfers between devices with their start and end apart: 29 -> 29, of which waited for: 20 -> 21; matrix products, arithmetic and copies ran while one was open for 5% -> 5% of each run, Pallas kernels for 9% -> 10%
where the time goes in v1:
time: 324 us; the launch traced here: 319 us
  waiting for transfers between devices  116 us (36%)
  Pallas kernels  95.7 us (30%)
  starting transfers between devices  47.5 us (15%)
  blocking collectives  20.8 us (6%)
  other arithmetic  15.1 us (5%)
  between operations  14.6 us (5%)
  local copies, waits for them, and re-layouts  8.47 us (3%)
    all_gather x1, waiting for transfers between devices, shards(): weight = lax.all_gather(half, ('fsdp', 'section'), axis=0, tiled=True)  48 us
    pallas_call x1, Pallas kernels, run_turn(): pl.pallas_call(turn_kernel, out_shape=[shape_of(ALL_TOKENS)] * 2 + saved,...  22.8 us
    all_gather x1, blocking collectives, shards(): small = lax.all_gather(from_home(small), 'fsdp', axis=0, tiled=False)  20.8 us
    pallas_call x2, Pallas kernels, add_halves(): pl.pallas_call(add_kernel, out_shape=shape_of(dims), grid=(12,), in_specs...  19.6 us
    pallas_call x1, Pallas kernels, run_self(): pl.pallas_call(self_kernel, out_shape=[shape_of(ALL_TOKENS), shape_of((1,...  13.4 us
    pallas_call x1, Pallas kernels, run_hidden(): pl.pallas_call(hidden_kernel, out_shape=[shape_of(ALL_TOKENS, jnp.float32...  13.4 us
    reduce_scatter x3, waiting for transfers between devices, scatter(): lax.psum_scatter(value, ('section', 'fsdp'), scatter_dimension=0, axis_in...  12.8 us
    pallas_call x1, Pallas kernels, run_first(): pl.pallas_call(first_kernel, out_shape=outs, in_specs=in_vmem(5) + [pl.Bl...  12.8 us
  transfers between devices with their start and end apart: 29, of which 21 were waited for; matrix products, arithmetic and copies ran while one was open for 5% of the time, Pallas kernels for 10%

profile of v1, /device:TPU:1, one launch (start us, length us, event | category | flops | bytes accessed | tf_op | source)
XLA Modules:
  0.0 318.8 jit_solution(13358953588640567471)
XLA Ops:
  7.3 4.2 %pack_weights.1 = (bf16[48,6144]{1,0:T(8,128)(2,1)}, bf16[48,6144]{1,0:T(8,128)(2,1)}) custom-call(bf16[48,768]{1,0:T(8,128)(2,1)} %bitcast.92, bf16[48,2,768]{2,1,0:T(2,128)(2,1)} %bitcast.88, bf16[48,768]{1,0:T(8,128)(2,1)} %bitcast.93, bf16[48,768]{1,0:T(8,128)(2,1)} %bitcast.94, bf16[48,2,768]{2,1,0:T(2,128)(2,1)} %bitcast.89, bf16[48,768]{1,0:T(8,128)(2,1)} %bitcast.95, ...), custom_call_target="tpu_custom_call" | custom-call | tf_op jit(solution)/shard_map/pack_weights/pallas_call | solution.py:757
  11.5 1.4 collective-permute-start
  12.9 1.8 collective-permute-done
  14.7 0.9 broadcast_select_fusion.2
  15.8 1.3 collective-permute-start.3
  17.4 1.3 collective-permute-start.4
  18.8 1.3 collective-permute-start.1
  20.1 1.3 collective-permute-start.2
  22.0 20.8 %all-gather = bf16[128,128]{1,0:T(8,128)(2,1)S(1)} all-gather(bf16[8,128]{1,0:T(8,128)(2,1)S(1)} %broadcast_select_fusion.19), channel_id=2, replica_groups=mesh['section'=2,'fsdp'=16,'rep'=4] {'fsdp'}, dimensions={0}, use_global_device_ids=true | all-gather | bytes 34816 | tf_op jit(solution)/shard_map/all_gather | solution.py:930
  44.7 1.0 bitcast_select_fusion.self_add_ref
  45.7 0.7 compare_select_fusion.cross_add_ref
  46.4 1.0 broadcast_select_fusion.4
  47.5 0.8 slice_bitcast_fusion
  48.2 1.0 broadcast_select_fusion.1.enc_ref
  49.2 48.0 %all-gather.3.cloned.1.call-done = bf16[1536,6144]{1,0:T(8,128)(2,1)} async-done(((bf16[48,6144]{1,0:T(8,128)(2,1)}), bf16[1536,6144]{1,0:T(8,128)(2,1)}) %all-gather.3.cloned.1.call-update) | async-done | bytes 18874384 | tf_op jit(solution)/shard_map/all_gather | solution.py:925
  97.3 12.8 %first_forward.1 = (bf16[128,768]{1,0:T(8,128)(2,1)}, bf16[512,768]{1,0:T(8,128)(2,1)}, bf16[512,768]{1,0:T(8,128)(2,1)}) custom-call(bf16[128,768]{1,0:T(8,128)(2,1)} %get-tuple-element.131.x_ref, bf16[512,768]{1,0:T(8,128)(2,1)} %broadcast_select_fusion.1.enc_ref, f32[2,768,64]{2,1,0:T(8,128)} %bitcast_select_fusion.self_add_ref, ...), custom_call_target="tpu_custom_call" | custom-call | tf_op jit(solution)/shard_map/first_forward/pallas_call | solution.py:624
  110.1 3.7 %collective-permute-start.5 = (bf16[128,768]{1,0:T(8,128)(2,1)}, bf16[128,768]{1,0:T(8,128)(2,1)S(1)}, u32[]{:S(2)}, u32[]{:S(2)}) collective-permute-start(bf16[128,768]{1,0:T(8,128)(2,1)} %get-tuple-element.137), channel_id=1, source_target_pairs={{0,1},{2,3},{4,5},{6,7},{8,9},{10,11},{12,13},{14,15},{16,17},{18,... | collective-permute-start | bytes 589832 | tf_op jit(solution)/shard_map/ppermute | solution.py:897
  113.7 3.8 %collective-permute-done.5 = bf16[128,768]{1,0:T(8,128)(2,1)S(1)} collective-permute-done((bf16[128,768]{1,0:T(8,128)(2,1)}, bf16[128,768]{1,0:T(8,128)(2,1)S(1)}, u32[]{:S(2)}, u32[]{:S(2)}) %collective-permute-start.5) | collective-permute-done | bytes 196640 | tf_op jit(solution)/shard_map/ppermute | solution.py:897
  118.2 22.8 %forward_and_back.1 = (bf16[128,768]{1,0:T(8,128)(2,1)}, bf16[128,768]{1,0:T(8,128)(2,1)}, bf16[128,768]{1,0:T(8,128)(2,1)}, bf16[128,768]{1,0:T(8,128)(2,1)}, b...) custom-call(bf16[128,768]{1,0:T(8,128)(2,1)} %broadcast_select_fusio, ...), custom_call_target="tpu_custom_call" | custom-call | tf_op jit(solution)/shard_map/forward_and_back/pallas_call | solution.py:639
  141.1 1.3 collective-permute-start.6
  142.4 6.2 %collective-permute-done.6 = bf16[128,768]{1,0:T(8,128)(2,1)S(1)} collective-permute-done((bf16[128,768]{1,0:T(8,128)(2,1)}, bf16[128,768]{1,0:T(8,128)(2,1)S(1)}, u32[]{:S(2)}, u32[]{:S(2)}) %collective-permute-start.6) | collective-permute-done | bytes 196640 | tf_op jit(solution)/shard_map/ppermute | solution.py:897
  148.6 0.7 broadcast_select_fusion.16.c_ref
  149.3 13.4 %hidden_backward.1 = (f32[128,768]{1,0:T(8,128)}, f32[1,768]{1,0:T(1,128)}, bf16[4,4,48,3072]{3,2,1,0:T(8,128)(2,1)}, bf16[4,4,48,3072]{3,2,1,0:T(8,128)(2,1)}) custom-call(bf16[128,768]{1,0:T(8,128)(2,1)} %broadcast_select_fusion.16.c_ref, f32[128,768]{1,0:T(8,128)} %get-tuple-element.141.a3_ref, f32[3,768]{1,0:T(4,128)} %reshape.217.gains_ref, ...), custom_call_target="tpu_custom_call" | custom-call | tf_op jit(solution)/shard_map/hidden_backward/pallas_call | solution.py:661
  162.6 2.1 collective-permute-start.7
  164.7 7.9 %cross_backward.1 = (f32[128,768]{1,0:T(8,128)}, f32[1,768]{1,0:T(1,128)}, bf16[128,768]{1,0:T(8,128)(2,1)}, bf16[128,768]{1,0:T(8,128)(2,1)}, bf16[512,768]{1,0:T(8,128)(2,1)}, /*index=5*/bf16[512,768]{1,0:T(8,128)(2,1)}) custom-call(f32[128,768]{1,0:T(8,128)} %get-tuple-element.148.stream_ref, f32[3,768]{1,0:T(4,128)} %reshape.217.gains_ref, ...), custom_call_target="tpu_custom_call" | custom-call | tf_op jit(solution)/shard_map/cross_backward/pallas_call | solution.py:682
  172.6 9.8 %add_halves.2 = bf16[768,3072]{1,0:T(8,128)(2,1)} custom-call(bf16[768,3072]{1,0:T(8,128)(2,1)} %bitcast.67, bf16[768,3072]{1,0:T(8,128)(2,1)} %bitcast.23.right), custom_call_target="tpu_custom_call" | custom-call | tf_op jit(solution)/shard_map/add_halves/pallas_call | solution.py:774
  182.7 13.4 %self_backward.1 = (bf16[128,768]{1,0:T(8,128)(2,1)}, f32[1,768]{1,0:T(1,128)}, f32[768,64]{1,0:T(8,128)}, bf16[512,768]{1,0:T(8,128)(2,1)}, bf16[4,4,48,3072]{3...) custom-call(f32[128,768]{1,0:T(8,128)} %get-tuple-element.154.stream_ref, ...), custom_call_target="tpu_custom_call" | custom-call | tf_op jit(solution)/shard_map/self_backward/pallas_call | solution.py:702
  196.5 7.9 %collective-permute-done.8 = bf16[4,4,48,3072]{3,2,1,0:T(8,128)(2,1)} collective-permute-done((bf16[4,4,48,3072]{3,2,1,0:T(8,128)(2,1)}, bf16[4,4,48,3072]{3,2,1,0:T(8,128)(2,1)}, u32[]{:S(2)}, u32[]{:S(2)}) %collective-permute-start.8) | collective-permute-done | bytes 4718624 | tf_op jit(solution)/shard_map/ppermute | solution.py:874
  204.4 9.8 %add_halves.3 = bf16[768,3072]{1,0:T(8,128)(2,1)} custom-call(bf16[768,3072]{1,0:T(8,128)(2,1)} %bitcast.66, bf16[768,3072]{1,0:T(8,128)(2,1)} %bitcast.25.right), custom_call_target="tpu_custom_call" | custom-call | tf_op jit(solution)/shard_map/add_halves/pallas_call | solution.py:774
  214.3 0.8 copy-done.6
  215.3 1.9 collective-permute-start.14
  217.9 0.7 reshape.214
  219.4 1.2 collective-permute-done.9
  221.2 2.0 collective-permute-done.10
  223.3 2.2 collective-permute-start.11
  225.5 2.0 collective-permute-done.11
  227.5 1.2 collective-permute-start.12
  228.7 2.1 collective-permute-done.12
  230.8 2.6 collective-permute-start.13
  233.4 2.1 collective-permute-done.13
  236.2 12.8 %reduce-scatter.6.cloned.1.call-done = bf16[192,3072]{1,0:T(8,128)(2,1)} async-done(((bf16[768,3072]{1,0:T(8,128)(2,1)}), bf16[192,3072]{1,0:T(8,128)(2,1)}) %reduce-scatter.6.cloned.1.call-update) | async-done | bytes 1179664 | tf_op jit(solution)/shard_map/reduce_scatter | solution.py:905
  249.0 3.2 %pad_maximum_fusion = bf16[192,6144]{1,0:T(8,128)(2,1)} fusion(bf16[192,3072]{1,0:T(8,128)(2,1)} %reduce-scatter.6.cloned.1.call-done, bf16[192,3072]{1,0:T(8,128)(2,1)} %reduce-scatter.4.cloned.1.call-done), kind=kLoop, calls=%fused_computation | loop fusion | flops 4718592 | bytes 4718592 | tf_op jit(solution)/shard_map/concatenate | solution.py:978
  252.3 1.1 copy-done
  253.4 3.2 collective-permute-start.15
  256.6 8.9 %collective-permute-done.15 = bf16[512,768]{1,0:T(8,128)(2,1)S(1)} collective-permute-done((bf16[512,768]{1,0:T(8,128)(2,1)S(1)}, bf16[512,768]{1,0:T(8,128)(2,1)S(1)}, u32[]{:S(2)}, u32[]{:S(2)}) %collective-permute-start.15) | collective-permute-done | bytes 786464 | tf_op jit(solution)/shard_map/ppermute | solution.py:885
  265.4 1.3 convert_add_fusion
  266.7 1.3 collective-permute-start.16
  268.0 2.5 collective-permute-start.17
  270.5 2.1 collective-permute-done.17
  272.6 0.8 add.60
  273.4 3.1 collective-permute-start.18
  276.5 0.8 fusion.2
  279.1 1.3 broadcast_select_fusion
  280.5 1.1 broadcast_select_fusion.10
  281.6 1.5 collective-permute-start.19
  283.1 1.4 collective-permute-start.20
  284.5 4.0 %collective-permute-done.19 = bf16[48,3072]{1,0:T(8,128)(2,1)S(1)} collective-permute-done((bf16[48,3072]{1,0:T(8,128)(2,1)S(1)}, bf16[48,3072]{1,0:T(8,128)(2,1)S(1)}, u32[]{:S(2)}, u32[]{:S(2)}) %collective-permute-start.19) | collective-permute-done | bytes 294944 | tf_op jit(solution)/shard_map/ppermute | solution.py:1001
  288.7 2.7 collective-permute-start.21
  291.4 1.8 collective-permute-start.23
  293.2 4.4 %collective-permute-done.21 = bf16[48,3072]{1,0:T(8,128)(2,1)S(1)} collective-permute-done((bf16[48,3072]{1,0:T(8,128)(2,1)S(1)}, bf16[48,3072]{1,0:T(8,128)(2,1)S(1)}, u32[]{:S(2)}, u32[]{:S(2)}) %collective-permute-start.21) | collective-permute-done | bytes 294944 | tf_op jit(solution)/shard_map/ppermute | solution.py:1005
  297.6 3.8 %collective-permute-done.22 = bf16[48,3072]{1,0:T(8,128)(2,1)S(1)} collective-permute-done((bf16[48,3072]{1,0:T(8,128)(2,1)S(1)}, bf16[48,3072]{1,0:T(8,128)(2,1)S(1)}, u32[]{:S(2)}, u32[]{:S(2)}) %collective-permute-start.22) | collective-permute-done | bytes 294944 | tf_op jit(solution)/shard_map/ppermute | solution.py:1004
  301.8 6.8 %collective-permute-start.24 = (bf16[48,6144]{1,0:T(8,128)(2,1)S(1)}, bf16[48,6144]{1,0:T(8,128)(2,1)S(1)}, u32[]{:S(2)}, u32[]{:S(2)}) collective-permute-start(bf16[48,6144]{1,0:T(8,128)(2,1)S(1)} %pad_maximum_fusion.2), channel_id=1, source_target_pairs={{0,64},{64,0},{1,65},{65,1},{2,66},{66,2},{3,67},{67,3},{4,68},{68... | collective-permute-start | bytes 1769480 | tf_op jit(solution)/shard_map/ppermute | solution.py:874
  308.6 1.6 collective-permute-done.24.theirs
  310.2 1.7 unpack_gradients.1
  (105 shorter events, 9.7 us)
Async XLA Ops:
  7.2 90.1 %all-gather.3.cloned.1.call-start = ((), (), s32[]{:S(2)}) async-start(), calls=%async_computation.3 | async-start | bytes 19464192 | tf_op jit(solution)/shard_map/all_gather | solution.py:925
  7.2 8.5 %copy-start.14 = (s32[2,1,256]{2,1,0:T(1,128)S(1)}, s32[2,1,256]{2,1,0:T(1,128)}, u32[]{:S(2)}) copy-start(s32[2,1,256]{2,1,0:T(1,128)} %param.29) | copy-start | bytes 6148
  7.2 8.5 %copy-start.10 = (s32[2,1,64]{2,1,0:T(1,128)S(1)}, s32[2,1,64]{2,1,0:T(1,128)}, u32[]{:S(2)}) copy-start(s32[2,1,64]{2,1,0:T(1,128)} %param.28) | copy-start | bytes 1540
  7.2 9.8 %copy-start.15 = (bf16[1,3,48]{2,1,0:T(4,128)(2,1)S(1)}, bf16[1,3,48]{2,1,0:T(4,128)(2,1)}, u32[]{:S(2)}) copy-start(bf16[1,3,48]{2,1,0:T(4,128)(2,1)} %param.30) | copy-start | bytes 868
  7.3 9.8 %copy-start.16 = (bf16[1,2,12]{2,1,0:T(2,128)(2,1)S(1)}, bf16[1,2,12]{2,1,0:T(2,128)(2,1)}, u32[]{:S(2)}) copy-start(bf16[1,2,12]{2,1,0:T(2,128)(2,1)} %param.34) | copy-start | bytes 148
  7.3 11.4 %copy-start.4 = (bf16[2,1,64,768]{3,2,1,0:T(8,128)(2,1)S(1)}, bf16[2,1,64,768]{3,2,1,0:T(8,128)(2,1)}, u32[]{:S(2)}) copy-start(bf16[2,1,64,768]{3,2,1,0:T(8,128)(2,1)} %param.26) | copy-start | bytes 589828
  7.3 11.4 %copy-start.5 = (bf16[2,1,64,768]{3,2,1,0:T(8,128)(2,1)S(1)}, bf16[2,1,64,768]{3,2,1,0:T(8,128)(2,1)}, u32[]{:S(2)}) copy-start(bf16[2,1,64,768]{3,2,1,0:T(8,128)(2,1)} %param.25) | copy-start | bytes 589828
  11.5 3.3 %collective-permute-start = (bf16[48,6144]{1,0:T(8,128)(2,1)}, bf16[48,6144]{1,0:T(8,128)(2,1)S(1)}, u32[]{:S(2)}, u32[]{:S(2)}) collective-permute-start(bf16[48,6144]{1,0:T(8,128)(2,1)} %get-tuple-element.129), channel_id=1, source_target_pairs={{0,64},{64,0},{1,65},{65,1},{2,66},{66,2},{3,67},{67,3},{4,68},{68... | collective-permute-start | bytes 1769480 | tf_op jit(solution)/shard_map/ppermute | solution.py:874
  14.7 5.3 %copy-start.3 = (bf16[2,1,256,768]{3,2,1,0:T(8,128)(2,1)S(1)}, bf16[2,1,256,768]{3,2,1,0:T(8,128)(2,1)}, u32[]{:S(2)}) copy-start(bf16[2,1,256,768]{3,2,1,0:T(8,128)(2,1)} %param.27) | copy-start | bytes 2359300
  14.7 28.1 %copy-start.9 = (f32[32,64]{1,0:T(8,128)S(1)}, f32[32,64]{1,0:T(8,128)}, u32[]{:S(2)}) copy-start(f32[32,64]{1,0:T(8,128)} %constant.143.clone) | copy-start | bytes 24580
  15.6 220.6 %reduce-scatter.4.cloned.1.call-start = ((), (), s32[]{:S(2)}) async-start(), calls=%async_computation.4 | async-start | bytes 5898240 | tf_op jit(solution)/shard_map/reduce_scatter | solution.py:905
  15.8 28.7 %collective-permute-start.3 = (s32[2,320]{1,0:T(2,128)S(1)}, s32[2,320]{1,0:T(2,128)S(1)}, u32[]{:S(2)}, u32[]{:S(2)}) collective-permute-start(s32[2,320]{1,0:T(2,128)S(1)} %pad_add_fusion), channel_id=1, source_target_pairs={{0,1},{65,64},{2,3},{67,66},{4,5},{69,68},{6,7},{71,70},{8,9},{73,... | collective-permute-start | bytes 7688 | tf_op jit(solution)/shard_map/ppermute | solution.py:889
  17.4 4.6 %collective-permute-start.4 = (bf16[8,128]{1,0:T(8,128)(2,1)S(1)}, bf16[8,128]{1,0:T(8,128)(2,1)S(1)}, u32[]{:S(2)}, u32[]{:S(2)}) collective-permute-start(bf16[8,128]{1,0:T(8,128)(2,1)S(1)} %scatter.15), channel_id=1, source_target_pairs={{0,64},{65,1},{2,66},{67,3},{4,68},{69,5},{6,70},{71,7},{8,72},{73... | collective-permute-start | bytes 6152 | tf_op jit(solution)/shard_map/ppermute | solution.py:878
  18.8 27.6 %collective-permute-start.1 = (bf16[2,128,768]{2,1,0:T(8,128)(2,1)S(1)}, bf16[2,128,768]{2,1,0:T(8,128)(2,1)}, u32[]{:S(2)}, u32[]{:S(2)}) collective-permute-start(bf16[2,128,768]{2,1,0:T(8,128)(2,1)S(1)} %pad_maximum_fusion.3), channel_id=1, source_target_pairs={{0,1},{65,64},{2,3},{67,66},{4,5},{69,68},{6,7},{71,70},{8,9},{73,... | collective-permute-start | bytes 1179656 | tf_op jit(solution)/shard_map/ppermute | solution.py:889
  20.1 28.2 %collective-permute-start.2 = (bf16[512,768]{1,0:T(8,128)(2,1)S(1)}, bf16[512,768]{1,0:T(8,128)(2,1)S(1)}, u32[]{:S(2)}, u32[]{:S(2)}) collective-permute-start(bf16[512,768]{1,0:T(8,128)(2,1)S(1)} %bitcast.74), channel_id=1, source_target_pairs={{0,1},{65,64},{2,3},{67,66},{4,5},{69,68},{6,7},{71,70},{8,9},{73,... | collective-permute-start | bytes 2359304 | tf_op jit(solution)/shard_map/ppermute | solution.py:889
  97.3 20.2 %copy-start.2 = (bf16[128,768]{1,0:T(8,128)(2,1)S(1)}, bf16[128,768]{1,0:T(8,128)(2,1)}, u32[]{:S(2)}) copy-start(bf16[128,768]{1,0:T(8,128)(2,1)} %get-tuple-element.131.x_ref) | copy-start | bytes 589828
  110.1 7.5 %collective-permute-start.5 = (bf16[128,768]{1,0:T(8,128)(2,1)}, bf16[128,768]{1,0:T(8,128)(2,1)S(1)}, u32[]{:S(2)}, u32[]{:S(2)}) collective-permute-start(bf16[128,768]{1,0:T(8,128)(2,1)} %get-tuple-element.137), channel_id=1, source_target_pairs={{0,1},{2,3},{4,5},{6,7},{8,9},{10,11},{12,13},{14,15},{16,17},{18,... | collective-permute-start | bytes 589832 | tf_op jit(solution)/shard_map/ppermute | solution.py:897
  118.2 30.3 %copy-start.1 = (bf16[128,768]{1,0:T(8,128)(2,1)S(1)}, bf16[128,768]{1,0:T(8,128)(2,1)}, u32[]{:S(2)}) copy-start(bf16[128,768]{1,0:T(8,128)(2,1)} %get-tuple-element.130.c_ref) | copy-start | bytes 589828
  141.1 7.5 %collective-permute-start.6 = (bf16[128,768]{1,0:T(8,128)(2,1)}, bf16[128,768]{1,0:T(8,128)(2,1)S(1)}, u32[]{:S(2)}, u32[]{:S(2)}) collective-permute-start(bf16[128,768]{1,0:T(8,128)(2,1)} %get-tuple-element.140), channel_id=1, source_target_pairs={{1,0},{3,2},{5,4},{7,6},{9,8},{11,10},{13,12},{15,14},{17,16},{19,... | collective-permute-start | bytes 589832 | tf_op jit(solution)/shard_map/ppermute | solution.py:897
  162.6 10.0 %collective-permute-start.7 = (bf16[4,4,48,3072]{3,2,1,0:T(8,128)(2,1)}, bf16[4,4,48,3072]{3,2,1,0:T(8,128)(2,1)}, u32[]{:S(2)}, u32[]{:S(2)}) collective-permute-start(bf16[4,4,48,3072]{3,2,1,0:T(8,128)(2,1)} %get-tuple-element.147), channel_id=1, source_target_pairs={{0,64},{64,0},{1,65},{65,1},{2,66},{66,2},{3,67},{67,3},{4,68},{68... | collective-permute-start | bytes 14155784 | tf_op jit(solution)/shard_map/ppermute | solution.py:874
  182.4 66.6 %reduce-scatter.6.cloned.1.call-start = ((), (), s32[]{:S(2)}) async-start(), calls=%async_computation.5 | async-start | bytes 5898240 | tf_op jit(solution)/shard_map/reduce_scatter | solution.py:905
  196.1 8.3 %collective-permute-start.8 = (bf16[4,4,48,3072]{3,2,1,0:T(8,128)(2,1)}, bf16[4,4,48,3072]{3,2,1,0:T(8,128)(2,1)}, u32[]{:S(2)}, u32[]{:S(2)}) collective-permute-start(bf16[4,4,48,3072]{3,2,1,0:T(8,128)(2,1)} %get-tuple-element.168), channel_id=1, source_target_pairs={{0,64},{64,0},{1,65},{65,1},{2,66},{66,2},{3,67},{67,3},{4,68},{68... | collective-permute-start | bytes 14155784 | tf_op jit(solution)/shard_map/ppermute | solution.py:874
  214.3 0.9 copy-start.6
  214.3 1.0 copy-start.7
  214.3 3.0 copy-start.8
  214.3 66.2 %reduce-scatter.8.cloned.1.call-start = ((), (), s32[]{:S(2)}) async-start(), calls=%async_computation.6 | async-start | bytes 2949120 | tf_op jit(solution)/shard_map/reduce_scatter | solution.py:905
  215.3 20.8 %collective-permute-start.14 = (bf16[2,128,768]{2,1,0:T(8,128)(2,1)S(1)}, bf16[2,128,768]{2,1,0:T(8,128)(2,1)S(1)}, u32[]{:S(2)}, u32[]{:S(2)}) collective-permute-start(bf16[2,128,768]{2,1,0:T(8,128)(2,1)S(1)} %pad_maximum_fusion.4), channel_id=1, source_target_pairs={{64,1},{1,64},{66,3},{3,66},{68,5},{5,68},{70,7},{7,70},{72,9},{9,... | collective-permute-start | bytes 1179656 | tf_op jit(solution)/shard_map/ppermute | solution.py:893
  217.5 1.5 copy-start.11
  217.5 1.5 copy-start.12
  217.5 1.5 copy-start.13
  219.3 1.3 collective-permute-start.9
  220.6 2.7 collective-permute-start.10
  223.3 4.2 %collective-permute-start.11 = (f32[8,768]{1,0:T(8,128)S(1)}, f32[8,768]{1,0:T(8,128)S(1)}, u32[]{:S(2)}, u32[]{:S(2)}) collective-permute-start(f32[8,768]{1,0:T(8,128)S(1)} %add.55), channel_id=1, source_target_pairs={{0,8},{4,12},{8,0},{12,4},{16,24},{20,28},{24,16},{28,20},{32,40},... | collective-permute-start | bytes 73736 | tf_op jit(solution)/shard_map/ppermute | solution.py:970
  227.5 3.3 %collective-permute-start.12 = (f32[8,768]{1,0:T(8,128)S(1)}, f32[8,768]{1,0:T(8,128)S(1)}, u32[]{:S(2)}, u32[]{:S(2)}) collective-permute-start(f32[8,768]{1,0:T(8,128)S(1)} %add.56), channel_id=1, source_target_pairs={{0,16},{4,20},{8,24},{12,28},{16,0},{20,4},{24,8},{28,12},{32,48},... | collective-permute-start | bytes 73736 | tf_op jit(solution)/shard_map/ppermute | solution.py:970
  230.8 4.7 %collective-permute-start.13 = (f32[8,768]{1,0:T(8,128)S(1)}, f32[8,768]{1,0:T(8,128)S(1)}, u32[]{:S(2)}, u32[]{:S(2)}) collective-permute-start(f32[8,768]{1,0:T(8,128)S(1)} %add.57), channel_id=1, source_target_pairs={{0,32},{4,36},{8,40},{12,44},{16,48},{20,52},{24,56},{28,60},{32,0... | collective-permute-start | bytes 73736 | tf_op jit(solution)/shard_map/ppermute | solution.py:970
  252.3 1.1 copy-start
  253.4 12.0 %collective-permute-start.15 = (bf16[512,768]{1,0:T(8,128)(2,1)S(1)}, bf16[512,768]{1,0:T(8,128)(2,1)S(1)}, u32[]{:S(2)}, u32[]{:S(2)}) collective-permute-start(bf16[512,768]{1,0:T(8,128)(2,1)S(1)} %copy-done), channel_id=1, source_target_pairs={{64,65},{1,0},{66,67},{3,2},{68,69},{5,4},{70,71},{7,6},{72,73},{9... | collective-permute-start | bytes 2359304 | tf_op jit(solution)/shard_map/ppermute | solution.py:885
  266.7 12.4 %collective-permute-start.16 = (f32[512,768]{1,0:T(8,128)}, f32[512,768]{1,0:T(8,128)S(1)}, u32[]{:S(2)}, u32[]{:S(2)}) collective-permute-start(f32[512,768]{1,0:T(8,128)} %convert_add_fusion), channel_id=1, source_target_pairs={{0,64},{65,1},{2,66},{67,3},{4,68},{69,5},{6,70},{71,7},{8,72},{73... | collective-permute-start | bytes 4718600 | tf_op jit(solution)/shard_map/ppermute | solution.py:878
  268.0 4.6 %collective-permute-start.17 = (f32[8,768]{1,0:T(8,128)}, f32[8,768]{1,0:T(8,128)}, u32[]{:S(2)}, u32[]{:S(2)}) collective-permute-start(f32[8,768]{1,0:T(8,128)} %add.58), channel_id=1, source_target_pairs={{0,2},{1,3},{2,0},{3,1},{4,6},{5,7},{6,4},{7,5},{8,10},{9,11},{10,... | collective-permute-start | bytes 73736 | tf_op jit(solution)/shard_map/ppermute | solution.py:970
  273.4 4.4 %collective-permute-start.18 = (f32[8,768]{1,0:T(8,128)S(1)}, f32[8,768]{1,0:T(8,128)S(1)}, u32[]{:S(2)}, u32[]{:S(2)}) collective-permute-start(f32[8,768]{1,0:T(8,128)S(1)} %add.60), channel_id=1, source_target_pairs={{0,1},{1,0},{2,3},{3,2},{4,5},{5,4},{6,7},{7,6},{8,9},{9,8},{10,11... | collective-permute-start | bytes 73736 | tf_op jit(solution)/shard_map/ppermute | solution.py:881
  281.6 7.0 %collective-permute-start.19 = (bf16[48,3072]{1,0:T(8,128)(2,1)S(1)}, bf16[48,3072]{1,0:T(8,128)(2,1)S(1)}, u32[]{:S(2)}, u32[]{:S(2)}) collective-permute-start(bf16[48,3072]{1,0:T(8,128)(2,1)S(1)} %get-tuple-element.225), channel_id=1, source_target_pairs={{0,1},{1,2},{2,3},{3,0},{4,5},{5,6},{6,7},{7,4},{8,9},{9,10},{10,1... | collective-permute-start | bytes 884744 | tf_op jit(solution)/shard_map/ppermute | solution.py:1001
  283.1 5.6 %collective-permute-start.20 = (bf16[48,3072]{1,0:T(8,128)(2,1)S(1)}, bf16[48,3072]{1,0:T(8,128)(2,1)S(1)}, u32[]{:S(2)}, u32[]{:S(2)}) collective-permute-start(bf16[48,3072]{1,0:T(8,128)(2,1)S(1)} %get-tuple-element.226), channel_id=1, source_target_pairs={{0,3},{1,0},{2,1},{3,2},{4,7},{5,4},{6,5},{7,6},{8,11},{9,8},{10,9... | collective-permute-start | bytes 884744 | tf_op jit(solution)/shard_map/ppermute | solution.py:1002
  288.7 8.9 %collective-permute-start.21 = (bf16[48,3072]{1,0:T(8,128)(2,1)S(1)}, bf16[48,3072]{1,0:T(8,128)(2,1)S(1)}, u32[]{:S(2)}, u32[]{:S(2)}) collective-permute-start(bf16[48,3072]{1,0:T(8,128)(2,1)S(1)} %add_convert_fusion), channel_id=1, source_target_pairs={{0,3},{1,0},{2,1},{3,2},{4,7},{5,4},{6,5},{7,6},{8,11},{9,8},{10,9... | collective-permute-start | bytes 884744 | tf_op jit(solution)/shard_map/ppermute | solution.py:1005
  291.4 10.0 %collective-permute-start.22 = (bf16[48,3072]{1,0:T(8,128)(2,1)S(1)}, bf16[48,3072]{1,0:T(8,128)(2,1)S(1)}, u32[]{:S(2)}, u32[]{:S(2)}) collective-permute-start(bf16[48,3072]{1,0:T(8,128)(2,1)S(1)} %add_convert_fusion), channel_id=1, source_target_pairs={{0,1},{1,2},{2,3},{3,0},{4,5},{5,6},{6,7},{7,4},{8,9},{9,10},{10,1... | collective-permute-start | bytes 884744 | tf_op jit(solution)/shard_map/ppermute | solution.py:1004
  291.4 10.2 %collective-permute-start.23 = (bf16[48,3072]{1,0:T(8,128)(2,1)S(1)}, bf16[48,3072]{1,0:T(8,128)(2,1)S(1)}, u32[]{:S(2)}, u32[]{:S(2)}) collective-permute-start(bf16[48,3072]{1,0:T(8,128)(2,1)S(1)} %add_convert_fusion), channel_id=1, source_target_pairs={{0,2},{1,3},{2,0},{3,1},{4,6},{5,7},{6,4},{7,5},{8,10},{9,11},{10,... | collective-permute-start | bytes 884744 | tf_op jit(solution)/shard_map/ppermute | solution.py:1006
  301.8 8.5 %collective-permute-start.24 = (bf16[48,6144]{1,0:T(8,128)(2,1)S(1)}, bf16[48,6144]{1,0:T(8,128)(2,1)S(1)}, u32[]{:S(2)}, u32[]{:S(2)}) collective-permute-start(bf16[48,6144]{1,0:T(8,128)(2,1)S(1)} %pad_maximum_fusion.2), channel_id=1, source_target_pairs={{0,64},{64,0},{1,65},{65,1},{2,66},{66,2},{3,67},{67,3},{4,68},{68... | collective-permute-start | bytes 1769480 | tf_op jit(solution)/shard_map/ppermute | solution.py:874
Sparse Core Ops, SparseCore 0:
  15.8 81.4 all-gather.2
  182.5 31.1 reduce-scatter.3
  216.1 32.8 reduce-scatter.5
  252.4 23.3 reduce-scatter.7

commit v2 on v1

--- a/solution.py
+++ b/solution.py
@@ -770,11 +770,11 @@
 
 def add_halves(keep, received):
     dims = (WIDE, ATT // 2)
-    spec = pl.BlockSpec((64, ATT // 2), lambda place: (place, 0))
+    spec = pl.BlockSpec((256, ATT // 2), lambda place: (place, 0))
     return pl.pallas_call(
         add_kernel,
         out_shape=shape_of(dims),
-        grid=(12,),
+        grid=(3,),
         in_specs=[spec, spec],
         out_specs=spec,
         compiler_params=params,
@@ -972,11 +972,10 @@
 
     little = add_pairs(add_pairs(little, "section", (1,)), "fsdp", (1, 2, 4, 8))
     outs = rows_back(jnp.stack([result, grad_input]))
-    wide_part, square_part, little, outs, grad_enc = lax.optimization_barrier(
-        (wide_part, square_part, little, outs, grad_enc)
+    wide_part, square_part, little, outs, other_enc = lax.optimization_barrier(
+        (wide_part, square_part, little, outs, to_home(grad_enc))
     )
     partial = scatter(jnp.concatenate([wide_part, square_part], axis=1), second_rings)
-    other_enc = to_home(grad_enc)
     little = add_pairs(little, "rep", (2,))
     little = jnp.where(at_home, little, beside(little))
     own_gains = lax.dynamic_slice(little, (0, part_index * ROWS_OWN), (3, ROWS_OWN))

time: 324 us -> 317 us (0.978)
  Pallas kernels: 95.7 us -> 90.2 us
    ppermute x1, waiting for transfers between devices: 8.87 us -> 0.01 us  [to_home(): return lax.ppermute(value, ('section', 'rep'), pairs)]
    pallas_call x2, Pallas kernels: 19.6 us -> 14 us  [add_halves(): pl.pallas_call(add_kernel, out_shape=shape_of(dims), grid=(3,), in_specs=...]
    reduce_scatter x3, waiting for transfers between devices: 12.8 us -> 18.4 us  [scatter(): lax.psum_scatter(value, ('section', 'fsdp'), scatter_dimension=0, axis_in...]
  transfers between devices with their start and end apart: 29 -> 29, of which waited for: 21 -> 19; matrix products, arithmetic and copies ran while one was open for 5% -> 5% of each run, Pallas kernels for 10% -> 9%
where the time goes in v2:
time: 317 us; the launch traced here: 312 us
  waiting for transfers between devices  115 us (36%)
  Pallas kernels  90.2 us (28%)
  starting transfers between devices  46.3 us (15%)
  blocking collectives  21.4 us (7%)
  other arithmetic  16.9 us (5%)
  between operations  14.6 us (5%)
  local copies, waits for them, and re-layouts  7.5 us (2%)
    all_gather x1, waiting for transfers between devices, shards(): weight = lax.all_gather(half, ('fsdp', 'section'), axis=0, tiled=True)  47.3 us
    pallas_call x1, Pallas kernels, run_turn(): pl.pallas_call(turn_kernel, out_shape=[shape_of(ALL_TOKENS)] * 2 + saved,...  22.9 us
    all_gather x1, blocking collectives, shards(): small = lax.all_gather(from_home(small), 'fsdp', axis=0, tiled=False)  21.4 us
    reduce_scatter x3, waiting for transfers between devices, scatter(): lax.psum_scatter(value, ('section', 'fsdp'), scatter_dimension=0, axis_in...  18.4 us
    pallas_call x2, Pallas kernels, add_halves(): pl.pallas_call(add_kernel, out_shape=shape_of(dims), grid=(3,), in_specs=...  14 us
    pallas_call x1, Pallas kernels, run_self(): pl.pallas_call(self_kernel, out_shape=[shape_of(ALL_TOKENS), shape_of((1,...  13.4 us
    pallas_call x1, Pallas kernels, run_hidden(): pl.pallas_call(hidden_kernel, out_shape=[shape_of(ALL_TOKENS, jnp.float32...  13.4 us
    pallas_call x1, Pallas kernels, run_first(): pl.pallas_call(first_kernel, out_shape=outs, in_specs=in_vmem(5) + [pl.Bl...  12.8 us
  transfers between devices with their start and end apart: 29, of which 19 were waited for; matrix products, arithmetic and copies ran while one was open for 5% of the time, Pallas kernels for 9%

profile of v2, /device:TPU:1, one launch (start us, length us, event | category | flops | bytes accessed | tf_op | source)
XLA Modules:
  0.0 312.0 jit_solution(14568628126953751231)
XLA Ops:
  7.3 4.2 %pack_weights.1 = (bf16[48,6144]{1,0:T(8,128)(2,1)}, bf16[48,6144]{1,0:T(8,128)(2,1)}) custom-call(bf16[48,768]{1,0:T(8,128)(2,1)} %bitcast.92, bf16[48,2,768]{2,1,0:T(2,128)(2,1)} %bitcast.88, bf16[48,768]{1,0:T(8,128)(2,1)} %bitcast.93, bf16[48,768]{1,0:T(8,128)(2,1)} %bitcast.94, bf16[48,2,768]{2,1,0:T(2,128)(2,1)} %bitcast.89, bf16[48,768]{1,0:T(8,128)(2,1)} %bitcast.95, ...), custom_call_target="tpu_custom_call" | custom-call | tf_op jit(solution)/shard_map/pack_weights/pallas_call | solution.py:757
  11.5 1.4 collective-permute-start
  12.9 1.8 collective-permute-done
  14.7 0.9 broadcast_select_fusion.2
  15.8 1.3 collective-permute-start.3
  17.4 1.3 collective-permute-start.4
  18.7 0.8 pad_maximum_fusion.3
  19.5 1.3 collective-permute-start.1
  20.8 1.3 collective-permute-start.2
  22.1 21.4 %all-gather = bf16[128,128]{1,0:T(8,128)(2,1)S(1)} all-gather(bf16[8,128]{1,0:T(8,128)(2,1)S(1)} %broadcast_select_fusion.19), channel_id=2, replica_groups=mesh['section'=2,'fsdp'=16,'rep'=4] {'fsdp'}, dimensions={0}, use_global_device_ids=true | all-gather | bytes 34816 | tf_op jit(solution)/shard_map/all_gather | solution.py:930
  45.4 1.0 bitcast_select_fusion.self_add_ref
  46.4 0.7 compare_select_fusion.cross_add_ref
  47.1 1.0 broadcast_select_fusion.4
  48.2 0.8 slice_bitcast_fusion
  49.0 1.0 broadcast_select_fusion.1.enc_ref
  50.0 47.3 %all-gather.3.cloned.1.call-done = bf16[1536,6144]{1,0:T(8,128)(2,1)} async-done(((bf16[48,6144]{1,0:T(8,128)(2,1)}), bf16[1536,6144]{1,0:T(8,128)(2,1)}) %all-gather.3.cloned.1.call-update) | async-done | bytes 18874384 | tf_op jit(solution)/shard_map/all_gather | solution.py:925
  97.3 12.8 %first_forward.1 = (bf16[128,768]{1,0:T(8,128)(2,1)}, bf16[512,768]{1,0:T(8,128)(2,1)}, bf16[512,768]{1,0:T(8,128)(2,1)}) custom-call(bf16[128,768]{1,0:T(8,128)(2,1)} %get-tuple-element.131.x_ref, bf16[512,768]{1,0:T(8,128)(2,1)} %broadcast_select_fusion.1.enc_ref, f32[2,768,64]{2,1,0:T(8,128)} %bitcast_select_fusion.self_add_ref, ...), custom_call_target="tpu_custom_call" | custom-call | tf_op jit(solution)/shard_map/first_forward/pallas_call | solution.py:624
  110.0 3.3 %collective-permute-start.5 = (bf16[128,768]{1,0:T(8,128)(2,1)}, bf16[128,768]{1,0:T(8,128)(2,1)S(1)}, u32[]{:S(2)}, u32[]{:S(2)}) collective-permute-start(bf16[128,768]{1,0:T(8,128)(2,1)} %get-tuple-element.137), channel_id=1, source_target_pairs={{0,1},{2,3},{4,5},{6,7},{8,9},{10,11},{12,13},{14,15},{16,17},{18,... | collective-permute-start | bytes 589832 | tf_op jit(solution)/shard_map/ppermute | solution.py:897
  113.3 4.2 %collective-permute-done.5 = bf16[128,768]{1,0:T(8,128)(2,1)S(1)} collective-permute-done((bf16[128,768]{1,0:T(8,128)(2,1)}, bf16[128,768]{1,0:T(8,128)(2,1)S(1)}, u32[]{:S(2)}, u32[]{:S(2)}) %collective-permute-start.5) | collective-permute-done | bytes 196640 | tf_op jit(solution)/shard_map/ppermute | solution.py:897
  118.2 22.9 %forward_and_back.1 = (bf16[128,768]{1,0:T(8,128)(2,1)}, bf16[128,768]{1,0:T(8,128)(2,1)}, bf16[128,768]{1,0:T(8,128)(2,1)}, bf16[128,768]{1,0:T(8,128)(2,1)}, b...) custom-call(bf16[128,768]{1,0:T(8,128)(2,1)} %broadcast_select_fusio, ...), custom_call_target="tpu_custom_call" | custom-call | tf_op jit(solution)/shard_map/forward_and_back/pallas_call | solution.py:639
  141.1 1.3 collective-permute-start.6
  142.4 6.2 %collective-permute-done.6 = bf16[128,768]{1,0:T(8,128)(2,1)S(1)} collective-permute-done((bf16[128,768]{1,0:T(8,128)(2,1)}, bf16[128,768]{1,0:T(8,128)(2,1)S(1)}, u32[]{:S(2)}, u32[]{:S(2)}) %collective-permute-start.6) | collective-permute-done | bytes 196640 | tf_op jit(solution)/shard_map/ppermute | solution.py:897
  149.3 13.4 %hidden_backward.1 = (f32[128,768]{1,0:T(8,128)}, f32[1,768]{1,0:T(1,128)}, bf16[4,4,48,3072]{3,2,1,0:T(8,128)(2,1)}, bf16[4,4,48,3072]{3,2,1,0:T(8,128)(2,1)}) custom-call(bf16[128,768]{1,0:T(8,128)(2,1)} %broadcast_select_fusion.16.c_ref, f32[128,768]{1,0:T(8,128)} %get-tuple-element.141.a3_ref, f32[3,768]{1,0:T(4,128)} %reshape.217.gains_ref, ...), custom_call_target="tpu_custom_call" | custom-call | tf_op jit(solution)/shard_map/hidden_backward/pallas_call | solution.py:661
  162.7 2.1 collective-permute-start.7
  164.7 7.9 %cross_backward.1 = (f32[128,768]{1,0:T(8,128)}, f32[1,768]{1,0:T(1,128)}, bf16[128,768]{1,0:T(8,128)(2,1)}, bf16[128,768]{1,0:T(8,128)(2,1)}, bf16[512,768]{1,0:T(8,128)(2,1)}, /*index=5*/bf16[512,768]{1,0:T(8,128)(2,1)}) custom-call(f32[128,768]{1,0:T(8,128)} %get-tuple-element.148.stream_ref, f32[3,768]{1,0:T(4,128)} %reshape.217.gains_ref, ...), custom_call_target="tpu_custom_call" | custom-call | tf_op jit(solution)/shard_map/cross_backward/pallas_call | solution.py:682
  172.6 6.9 %add_halves.2 = bf16[768,3072]{1,0:T(8,128)(2,1)} custom-call(bf16[768,3072]{1,0:T(8,128)(2,1)} %bitcast.67, bf16[768,3072]{1,0:T(8,128)(2,1)} %bitcast.23.right), custom_call_target="tpu_custom_call" | custom-call | tf_op jit(solution)/shard_map/add_halves/pallas_call | solution.py:774
  180.1 13.4 %self_backward.1 = (bf16[128,768]{1,0:T(8,128)(2,1)}, f32[1,768]{1,0:T(1,128)}, f32[768,64]{1,0:T(8,128)}, bf16[512,768]{1,0:T(8,128)(2,1)}, bf16[4,4,48,3072]{3...) custom-call(f32[128,768]{1,0:T(8,128)} %get-tuple-element.154.stream_ref, ...), custom_call_target="tpu_custom_call" | custom-call | tf_op jit(solution)/shard_map/self_backward/pallas_call | solution.py:702
  193.9 7.9 %collective-permute-done.8 = bf16[4,4,48,3072]{3,2,1,0:T(8,128)(2,1)} collective-permute-done((bf16[4,4,48,3072]{3,2,1,0:T(8,128)(2,1)}, bf16[4,4,48,3072]{3,2,1,0:T(8,128)(2,1)}, u32[]{:S(2)}, u32[]{:S(2)}) %collective-permute-start.8) | collective-permute-done | bytes 4718624 | tf_op jit(solution)/shard_map/ppermute | solution.py:874
  201.8 7.0 %add_halves.3 = bf16[768,3072]{1,0:T(8,128)(2,1)} custom-call(bf16[768,3072]{1,0:T(8,128)(2,1)} %bitcast.66, bf16[768,3072]{1,0:T(8,128)(2,1)} %bitcast.25.right), custom_call_target="tpu_custom_call" | custom-call | tf_op jit(solution)/shard_map/add_halves/pallas_call | solution.py:774
  208.9 1.1 copy-done
  210.0 1.3 collective-permute-start.15
  211.4 4.5 %collective-permute-start.14 = (bf16[2,128,768]{2,1,0:T(8,128)(2,1)S(1)}, bf16[2,128,768]{2,1,0:T(8,128)(2,1)}, u32[]{:S(2)}, u32[]{:S(2)}) collective-permute-start(bf16[2,128,768]{2,1,0:T(8,128)(2,1)S(1)} %pad_maximum_fusion.4), channel_id=1, source_target_pairs={{64,1},{1,64},{66,3},{3,66},{68,5},{5,68},{70,7},{7,70},{72,9},{9,... | collective-permute-start | bytes 1179656 | tf_op jit(solution)/shard_map/ppermute | solution.py:893
  218.1 1.2 collective-permute-done.9
  219.9 2.3 collective-permute-done.10
  222.2 2.2 collective-permute-start.11
  224.4 2.1 collective-permute-done.11
  226.5 1.1 collective-permute-start.12
  227.7 2.2 collective-permute-done.12
  229.9 2.6 collective-permute-start.13
  232.5 2.2 collective-permute-done.13
  235.3 1.0 broadcast_select_fusion.3
  236.4 9.8 %reduce-scatter.6.cloned.1.call-done = bf16[192,3072]{1,0:T(8,128)(2,1)} async-done(((bf16[768,3072]{1,0:T(8,128)(2,1)}), bf16[192,3072]{1,0:T(8,128)(2,1)}) %reduce-scatter.6.cloned.1.call-update) | async-done | bytes 1179664 | tf_op jit(solution)/shard_map/reduce_scatter | solution.py:905
  246.2 3.2 %pad_maximum_fusion = bf16[192,6144]{1,0:T(8,128)(2,1)} fusion(bf16[192,3072]{1,0:T(8,128)(2,1)} %reduce-scatter.6.cloned.1.call-done, bf16[192,3072]{1,0:T(8,128)(2,1)} %reduce-scatter.4.cloned.1.call-done), kind=kLoop, calls=%fused_computation | loop fusion | flops 4718592 | bytes 4718592 | tf_op jit(solution)/shard_map/concatenate | solution.py:978
  249.5 1.3 convert_add_fusion
  250.8 1.3 collective-permute-start.16
  252.1 3.0 collective-permute-start.17
  255.1 1.8 collective-permute-done.17
  256.8 0.8 add.60
  257.6 2.8 collective-permute-start.18
  260.4 0.8 fusion.2
  261.1 0.8 collective-permute-done.18
  263.4 1.3 broadcast_select_fusion
  264.7 8.5 %reduce-scatter.8.cloned.1.call-done = bf16[48,6144]{1,0:T(8,128)(2,1)} async-done(((bf16[192,6144]{1,0:T(8,128)(2,1)}), bf16[48,6144]{1,0:T(8,128)(2,1)}) %reduce-scatter.8.cloned.1.call-update) | async-done | bytes 589840 | tf_op jit(solution)/shard_map/reduce_scatter | solution.py:905
  273.2 1.1 broadcast_select_fusion.10
  274.3 1.3 collective-permute-start.19
  275.6 1.5 collective-permute-start.20
  277.1 5.2 %collective-permute-done.19 = bf16[48,3072]{1,0:T(8,128)(2,1)S(1)} collective-permute-done((bf16[48,3072]{1,0:T(8,128)(2,1)S(1)}, bf16[48,3072]{1,0:T(8,128)(2,1)S(1)}, u32[]{:S(2)}, u32[]{:S(2)}) %collective-permute-start.19) | collective-permute-done | bytes 294944 | tf_op jit(solution)/shard_map/ppermute | solution.py:1000
  282.3 2.5 collective-permute-start.21
  284.8 1.3 collective-permute-start.23
  286.0 2.4 collective-permute-done.21
  288.4 6.8 %collective-permute-done.22 = bf16[48,3072]{1,0:T(8,128)(2,1)S(1)} collective-permute-done((bf16[48,3072]{1,0:T(8,128)(2,1)S(1)}, bf16[48,3072]{1,0:T(8,128)(2,1)S(1)}, u32[]{:S(2)}, u32[]{:S(2)}) %collective-permute-start.22) | collective-permute-done | bytes 294944 | tf_op jit(solution)/shard_map/ppermute | solution.py:1003
  295.9 6.0 %collective-permute-start.24 = (bf16[48,6144]{1,0:T(8,128)(2,1)S(1)}, bf16[48,6144]{1,0:T(8,128)(2,1)S(1)}, u32[]{:S(2)}, u32[]{:S(2)}) collective-permute-start(bf16[48,6144]{1,0:T(8,128)(2,1)S(1)} %pad_maximum_fusion.2), channel_id=1, source_target_pairs={{0,64},{64,0},{1,65},{65,1},{2,66},{66,2},{3,67},{67,3},{4,68},{68... | collective-permute-start | bytes 1769480 | tf_op jit(solution)/shard_map/ppermute | solution.py:874
  302.0 1.6 collective-permute-done.24.theirs
  303.6 1.7 unpack_gradients.1
  (105 shorter events, 10.3 us)
Async XLA Ops:
  7.2 90.1 %all-gather.3.cloned.1.call-start = ((), (), s32[]{:S(2)}) async-start(), calls=%async_computation.3 | async-start | bytes 19464192 | tf_op jit(solution)/shard_map/all_gather | solution.py:925
  7.2 8.5 %copy-start.14 = (s32[2,1,256]{2,1,0:T(1,128)S(1)}, s32[2,1,256]{2,1,0:T(1,128)}, u32[]{:S(2)}) copy-start(s32[2,1,256]{2,1,0:T(1,128)} %param.29) | copy-start | bytes 6148
  7.2 8.5 %copy-start.10 = (s32[2,1,64]{2,1,0:T(1,128)S(1)}, s32[2,1,64]{2,1,0:T(1,128)}, u32[]{:S(2)}) copy-start(s32[2,1,64]{2,1,0:T(1,128)} %param.28) | copy-start | bytes 1540
  7.2 9.8 %copy-start.15 = (bf16[1,3,48]{2,1,0:T(4,128)(2,1)S(1)}, bf16[1,3,48]{2,1,0:T(4,128)(2,1)}, u32[]{:S(2)}) copy-start(bf16[1,3,48]{2,1,0:T(4,128)(2,1)} %param.30) | copy-start | bytes 868
  7.3 9.8 %copy-start.16 = (bf16[1,2,12]{2,1,0:T(2,128)(2,1)S(1)}, bf16[1,2,12]{2,1,0:T(2,128)(2,1)}, u32[]{:S(2)}) copy-start(bf16[1,2,12]{2,1,0:T(2,128)(2,1)} %param.34) | copy-start | bytes 148
  7.3 11.4 %copy-start.4 = (bf16[2,1,64,768]{3,2,1,0:T(8,128)(2,1)S(1)}, bf16[2,1,64,768]{3,2,1,0:T(8,128)(2,1)}, u32[]{:S(2)}) copy-start(bf16[2,1,64,768]{3,2,1,0:T(8,128)(2,1)} %param.26) | copy-start | bytes 589828
  7.3 11.4 %copy-start.5 = (bf16[2,1,64,768]{3,2,1,0:T(8,128)(2,1)S(1)}, bf16[2,1,64,768]{3,2,1,0:T(8,128)(2,1)}, u32[]{:S(2)}) copy-start(bf16[2,1,64,768]{3,2,1,0:T(8,128)(2,1)} %param.25) | copy-start | bytes 589828
  11.5 3.3 %collective-permute-start = (bf16[48,6144]{1,0:T(8,128)(2,1)}, bf16[48,6144]{1,0:T(8,128)(2,1)S(1)}, u32[]{:S(2)}, u32[]{:S(2)}) collective-permute-start(bf16[48,6144]{1,0:T(8,128)(2,1)} %get-tuple-element.129), channel_id=1, source_target_pairs={{0,64},{64,0},{1,65},{65,1},{2,66},{66,2},{3,67},{67,3},{4,68},{68... | collective-permute-start | bytes 1769480 | tf_op jit(solution)/shard_map/ppermute | solution.py:874
  14.7 6.1 %copy-start.3 = (bf16[2,1,256,768]{3,2,1,0:T(8,128)(2,1)S(1)}, bf16[2,1,256,768]{3,2,1,0:T(8,128)(2,1)}, u32[]{:S(2)}) copy-start(bf16[2,1,256,768]{3,2,1,0:T(8,128)(2,1)} %param.27) | copy-start | bytes 2359300
  14.7 28.8 %copy-start.9 = (f32[32,64]{1,0:T(8,128)S(1)}, f32[32,64]{1,0:T(8,128)}, u32[]{:S(2)}) copy-start(f32[32,64]{1,0:T(8,128)} %constant.143.clone) | copy-start | bytes 24580
  15.6 220.7 %reduce-scatter.4.cloned.1.call-start = ((), (), s32[]{:S(2)}) async-start(), calls=%async_computation.4 | async-start | bytes 5898240 | tf_op jit(solution)/shard_map/reduce_scatter | solution.py:905
  15.8 29.4 %collective-permute-start.3 = (s32[2,320]{1,0:T(2,128)S(1)}, s32[2,320]{1,0:T(2,128)S(1)}, u32[]{:S(2)}, u32[]{:S(2)}) collective-permute-start(s32[2,320]{1,0:T(2,128)S(1)} %pad_add_fusion), channel_id=1, source_target_pairs={{0,1},{65,64},{2,3},{67,66},{4,5},{69,68},{6,7},{71,70},{8,9},{73,... | collective-permute-start | bytes 7688 | tf_op jit(solution)/shard_map/ppermute | solution.py:889
  17.4 4.7 %collective-permute-start.4 = (bf16[8,128]{1,0:T(8,128)(2,1)S(1)}, bf16[8,128]{1,0:T(8,128)(2,1)S(1)}, u32[]{:S(2)}, u32[]{:S(2)}) collective-permute-start(bf16[8,128]{1,0:T(8,128)(2,1)S(1)} %scatter.15), channel_id=1, source_target_pairs={{0,64},{65,1},{2,66},{67,3},{4,68},{69,5},{6,70},{71,7},{8,72},{73... | collective-permute-start | bytes 6152 | tf_op jit(solution)/shard_map/ppermute | solution.py:878
  19.5 27.6 %collective-permute-start.1 = (bf16[2,128,768]{2,1,0:T(8,128)(2,1)}, bf16[2,128,768]{2,1,0:T(8,128)(2,1)}, u32[]{:S(2)}, u32[]{:S(2)}) collective-permute-start(bf16[2,128,768]{2,1,0:T(8,128)(2,1)} %pad_maximum_fusion.3), channel_id=1, source_target_pairs={{0,1},{65,64},{2,3},{67,66},{4,5},{69,68},{6,7},{71,70},{8,9},{73,... | collective-permute-start | bytes 1179656 | tf_op jit(solution)/shard_map/ppermute | solution.py:889
  20.8 28.2 %collective-permute-start.2 = (bf16[512,768]{1,0:T(8,128)(2,1)S(1)}, bf16[512,768]{1,0:T(8,128)(2,1)S(1)}, u32[]{:S(2)}, u32[]{:S(2)}) collective-permute-start(bf16[512,768]{1,0:T(8,128)(2,1)S(1)} %bitcast.74), channel_id=1, source_target_pairs={{0,1},{65,64},{2,3},{67,66},{4,5},{69,68},{6,7},{71,70},{8,9},{73,... | collective-permute-start | bytes 2359304 | tf_op jit(solution)/shard_map/ppermute | solution.py:889
  97.2 20.3 %copy-start.2 = (bf16[128,768]{1,0:T(8,128)(2,1)S(1)}, bf16[128,768]{1,0:T(8,128)(2,1)}, u32[]{:S(2)}) copy-start(bf16[128,768]{1,0:T(8,128)(2,1)} %get-tuple-element.131.x_ref) | copy-start | bytes 589828
  110.0 7.5 %collective-permute-start.5 = (bf16[128,768]{1,0:T(8,128)(2,1)}, bf16[128,768]{1,0:T(8,128)(2,1)S(1)}, u32[]{:S(2)}, u32[]{:S(2)}) collective-permute-start(bf16[128,768]{1,0:T(8,128)(2,1)} %get-tuple-element.137), channel_id=1, source_target_pairs={{0,1},{2,3},{4,5},{6,7},{8,9},{10,11},{12,13},{14,15},{16,17},{18,... | collective-permute-start | bytes 589832 | tf_op jit(solution)/shard_map/ppermute | solution.py:897
  118.2 30.4 %copy-start.1 = (bf16[128,768]{1,0:T(8,128)(2,1)S(1)}, bf16[128,768]{1,0:T(8,128)(2,1)}, u32[]{:S(2)}) copy-start(bf16[128,768]{1,0:T(8,128)(2,1)} %get-tuple-element.130.c_ref) | copy-start | bytes 589828
  141.1 7.5 %collective-permute-start.6 = (bf16[128,768]{1,0:T(8,128)(2,1)}, bf16[128,768]{1,0:T(8,128)(2,1)S(1)}, u32[]{:S(2)}, u32[]{:S(2)}) collective-permute-start(bf16[128,768]{1,0:T(8,128)(2,1)} %get-tuple-element.140), channel_id=1, source_target_pairs={{1,0},{3,2},{5,4},{7,6},{9,8},{11,10},{13,12},{15,14},{17,16},{19,... | collective-permute-start | bytes 589832 | tf_op jit(solution)/shard_map/ppermute | solution.py:897
  162.7 10.0 %collective-permute-start.7 = (bf16[4,4,48,3072]{3,2,1,0:T(8,128)(2,1)}, bf16[4,4,48,3072]{3,2,1,0:T(8,128)(2,1)}, u32[]{:S(2)}, u32[]{:S(2)}) collective-permute-start(bf16[4,4,48,3072]{3,2,1,0:T(8,128)(2,1)} %get-tuple-element.147), channel_id=1, source_target_pairs={{0,64},{64,0},{1,65},{65,1},{2,66},{66,2},{3,67},{67,3},{4,68},{68... | collective-permute-start | bytes 14155784 | tf_op jit(solution)/shard_map/ppermute | solution.py:874
  179.6 66.6 %reduce-scatter.6.cloned.1.call-start = ((), (), s32[]{:S(2)}) async-start(), calls=%async_computation.5 | async-start | bytes 5898240 | tf_op jit(solution)/shard_map/reduce_scatter | solution.py:905
  193.5 8.3 %collective-permute-start.8 = (bf16[4,4,48,3072]{3,2,1,0:T(8,128)(2,1)}, bf16[4,4,48,3072]{3,2,1,0:T(8,128)(2,1)}, u32[]{:S(2)}, u32[]{:S(2)}) collective-permute-start(bf16[4,4,48,3072]{3,2,1,0:T(8,128)(2,1)} %get-tuple-element.168), channel_id=1, source_target_pairs={{0,64},{64,0},{1,65},{65,1},{2,66},{66,2},{3,67},{67,3},{4,68},{68... | collective-permute-start | bytes 14155784 | tf_op jit(solution)/shard_map/ppermute | solution.py:874
  208.9 1.2 copy-start
  208.9 2.5 copy-start.6
  208.9 2.5 copy-start.7
  208.9 7.0 %copy-start.8 = (f32[768,64]{1,0:T(8,128)S(1)}, f32[768,64]{1,0:T(8,128)}, u32[]{:S(2)}) copy-start(f32[768,64]{1,0:T(8,128)} %get-tuple-element.172) | copy-start | bytes 589828
  208.9 64.3 %reduce-scatter.8.cloned.1.call-start = ((), (), s32[]{:S(2)}) async-start(), calls=%async_computation.6 | async-start | bytes 2949120 | tf_op jit(solution)/shard_map/reduce_scatter | solution.py:905
  210.0 26.3 %collective-permute-start.15 = (bf16[512,768]{1,0:T(8,128)(2,1)S(1)}, bf16[512,768]{1,0:T(8,128)(2,1)S(1)}, u32[]{:S(2)}, u32[]{:S(2)}) collective-permute-start(bf16[512,768]{1,0:T(8,128)(2,1)S(1)} %copy-done), channel_id=1, source_target_pairs={{64,65},{1,0},{66,67},{3,2},{68,69},{5,4},{70,71},{7,6},{72,73},{9... | collective-permute-start | bytes 2359304 | tf_op jit(solution)/shard_map/ppermute | solution.py:885
  211.4 23.8 %collective-permute-start.14 = (bf16[2,128,768]{2,1,0:T(8,128)(2,1)S(1)}, bf16[2,128,768]{2,1,0:T(8,128)(2,1)}, u32[]{:S(2)}, u32[]{:S(2)}) collective-permute-start(bf16[2,128,768]{2,1,0:T(8,128)(2,1)S(1)} %pad_maximum_fusion.4), channel_id=1, source_target_pairs={{64,1},{1,64},{66,3},{3,66},{68,5},{5,68},{70,7},{7,70},{72,9},{9,... | collective-permute-start | bytes 1179656 | tf_op jit(solution)/shard_map/ppermute | solution.py:893
  216.1 1.5 copy-start.11
  216.1 1.5 copy-start.12
  216.1 1.5 copy-start.13
  218.0 1.3 collective-permute-start.9
  219.3 3.0 collective-permute-start.10
  222.2 4.3 %collective-permute-start.11 = (f32[8,768]{1,0:T(8,128)S(1)}, f32[8,768]{1,0:T(8,128)S(1)}, u32[]{:S(2)}, u32[]{:S(2)}) collective-permute-start(f32[8,768]{1,0:T(8,128)S(1)} %add.55), channel_id=1, source_target_pairs={{0,8},{4,12},{8,0},{12,4},{16,24},{20,28},{24,16},{28,20},{32,40},... | collective-permute-start | bytes 73736 | tf_op jit(solution)/shard_map/ppermute | solution.py:970
  226.5 3.3 %collective-permute-start.12 = (f32[8,768]{1,0:T(8,128)S(1)}, f32[8,768]{1,0:T(8,128)S(1)}, u32[]{:S(2)}, u32[]{:S(2)}) collective-permute-start(f32[8,768]{1,0:T(8,128)S(1)} %add.56), channel_id=1, source_target_pairs={{0,16},{4,20},{8,24},{12,28},{16,0},{20,4},{24,8},{28,12},{32,48},... | collective-permute-start | bytes 73736 | tf_op jit(solution)/shard_map/ppermute | solution.py:970
  229.9 4.8 %collective-permute-start.13 = (f32[8,768]{1,0:T(8,128)S(1)}, f32[8,768]{1,0:T(8,128)S(1)}, u32[]{:S(2)}, u32[]{:S(2)}) collective-permute-start(f32[8,768]{1,0:T(8,128)S(1)} %add.57), channel_id=1, source_target_pairs={{0,32},{4,36},{8,40},{12,44},{16,48},{20,52},{24,56},{28,60},{32,0... | collective-permute-start | bytes 73736 | tf_op jit(solution)/shard_map/ppermute | solution.py:970
  250.8 12.6 %collective-permute-start.16 = (f32[512,768]{1,0:T(8,128)}, f32[512,768]{1,0:T(8,128)S(1)}, u32[]{:S(2)}, u32[]{:S(2)}) collective-permute-start(f32[512,768]{1,0:T(8,128)} %convert_add_fusion), channel_id=1, source_target_pairs={{0,64},{65,1},{2,66},{67,3},{4,68},{69,5},{6,70},{71,7},{8,72},{73... | collective-permute-start | bytes 4718600 | tf_op jit(solution)/shard_map/ppermute | solution.py:878
  252.1 4.7 %collective-permute-start.17 = (f32[8,768]{1,0:T(8,128)}, f32[8,768]{1,0:T(8,128)}, u32[]{:S(2)}, u32[]{:S(2)}) collective-permute-start(f32[8,768]{1,0:T(8,128)} %add.58), channel_id=1, source_target_pairs={{0,2},{1,3},{2,0},{3,1},{4,6},{5,7},{6,4},{7,5},{8,10},{9,11},{10,... | collective-permute-start | bytes 73736 | tf_op jit(solution)/shard_map/ppermute | solution.py:970
  257.6 4.4 %collective-permute-start.18 = (f32[8,768]{1,0:T(8,128)S(1)}, f32[8,768]{1,0:T(8,128)S(1)}, u32[]{:S(2)}, u32[]{:S(2)}) collective-permute-start(f32[8,768]{1,0:T(8,128)S(1)} %add.60), channel_id=1, source_target_pairs={{0,1},{1,0},{2,3},{3,2},{4,5},{5,4},{6,7},{7,6},{8,9},{9,8},{10,11... | collective-permute-start | bytes 73736 | tf_op jit(solution)/shard_map/ppermute | solution.py:881
  274.3 7.9 %collective-permute-start.19 = (bf16[48,3072]{1,0:T(8,128)(2,1)S(1)}, bf16[48,3072]{1,0:T(8,128)(2,1)S(1)}, u32[]{:S(2)}, u32[]{:S(2)}) collective-permute-start(bf16[48,3072]{1,0:T(8,128)(2,1)S(1)} %get-tuple-element.225), channel_id=1, source_target_pairs={{0,1},{1,2},{2,3},{3,0},{4,5},{5,6},{6,7},{7,4},{8,9},{9,10},{10,1... | collective-permute-start | bytes 884744 | tf_op jit(solution)/shard_map/ppermute | solution.py:1000
  275.6 6.6 %collective-permute-start.20 = (bf16[48,3072]{1,0:T(8,128)(2,1)S(1)}, bf16[48,3072]{1,0:T(8,128)(2,1)S(1)}, u32[]{:S(2)}, u32[]{:S(2)}) collective-permute-start(bf16[48,3072]{1,0:T(8,128)(2,1)S(1)} %get-tuple-element.226), channel_id=1, source_target_pairs={{0,3},{1,0},{2,1},{3,2},{4,7},{5,4},{6,5},{7,6},{8,11},{9,8},{10,9... | collective-permute-start | bytes 884744 | tf_op jit(solution)/shard_map/ppermute | solution.py:1001
  282.3 6.1 %collective-permute-start.21 = (bf16[48,3072]{1,0:T(8,128)(2,1)S(1)}, bf16[48,3072]{1,0:T(8,128)(2,1)S(1)}, u32[]{:S(2)}, u32[]{:S(2)}) collective-permute-start(bf16[48,3072]{1,0:T(8,128)(2,1)S(1)} %add_convert_fusion), channel_id=1, source_target_pairs={{0,3},{1,0},{2,1},{3,2},{4,7},{5,4},{6,5},{7,6},{8,11},{9,8},{10,9... | collective-permute-start | bytes 884744 | tf_op jit(solution)/shard_map/ppermute | solution.py:1004
  284.8 10.5 %collective-permute-start.22 = (bf16[48,3072]{1,0:T(8,128)(2,1)S(1)}, bf16[48,3072]{1,0:T(8,128)(2,1)S(1)}, u32[]{:S(2)}, u32[]{:S(2)}) collective-permute-start(bf16[48,3072]{1,0:T(8,128)(2,1)S(1)} %add_convert_fusion), channel_id=1, source_target_pairs={{0,1},{1,2},{2,3},{3,0},{4,5},{5,6},{6,7},{7,4},{8,9},{9,10},{10,1... | collective-permute-start | bytes 884744 | tf_op jit(solution)/shard_map/ppermute | solution.py:1003
  284.8 11.0 %collective-permute-start.23 = (bf16[48,3072]{1,0:T(8,128)(2,1)S(1)}, bf16[48,3072]{1,0:T(8,128)(2,1)S(1)}, u32[]{:S(2)}, u32[]{:S(2)}) collective-permute-start(bf16[48,3072]{1,0:T(8,128)(2,1)S(1)} %add_convert_fusion), channel_id=1, source_target_pairs={{0,2},{1,3},{2,0},{3,1},{4,6},{5,7},{6,4},{7,5},{8,10},{9,11},{10,... | collective-permute-start | bytes 884744 | tf_op jit(solution)/shard_map/ppermute | solution.py:1005
  295.9 7.7 %collective-permute-start.24 = (bf16[48,6144]{1,0:T(8,128)(2,1)S(1)}, bf16[48,6144]{1,0:T(8,128)(2,1)S(1)}, u32[]{:S(2)}, u32[]{:S(2)}) collective-permute-start(bf16[48,6144]{1,0:T(8,128)(2,1)S(1)} %pad_maximum_fusion.2), channel_id=1, source_target_pairs={{0,64},{64,0},{1,65},{65,1},{2,66},{66,2},{3,67},{67,3},{4,68},{68... | collective-permute-start | bytes 1769480 | tf_op jit(solution)/shard_map/ppermute | solution.py:874
Sparse Core Ops, SparseCore 0:
  15.8 81.4 all-gather.2
  179.7 31.1 reduce-scatter.3
  213.3 32.8 reduce-scatter.5
  249.6 23.5 reduce-scatter.7
